TPU v7x, 256 devices: a whole 4x4x8 slice. The times are simulated.
256 devices in a mesh: param: 8 (over z_hi, core), slab: 8 (over x, z_lo), tile: 4 (over y).
Axes of the slice: x: 4, y: 4, z: 8 (z_hi: 4, z_lo: 2; z = z_hi * 2 + z_lo), core: 2. Of those that a mesh axis runs over, the one named last changes fastest.
Arguments:
- state: float32 [14, 24, 128, 128], P(None, 'slab', 'tile', 'param'), may hold values from 0 to 1
- sensitivity: float32 [64, 14, 24, 128, 128], P('param', None, 'slab', 'tile'), may hold values from -6 to 6
- packing: float32 [24, 128, 128], P('slab', 'tile'), may hold values from 0.5 to 2
- cell_zone: int32 [24, 128, 128], P('slab', 'tile'), may hold values from 0 to 7
- coefficients: float32 [8, 8], replicated, may hold values from 0.3 to 1.5
- param_target: int32 [64], P('param'), may hold values from 0 to 63
Outputs:
- new_state: float32 [14, 24, 128, 128], P(None, 'slab', 'tile', 'param')
- new_sensitivity: float32 [64, 14, 24, 128, 128], P('param', None, 'slab', 'tile')
Inputs may be any that keep to these rules, and one draw needn't show every extreme that they name: param_target[p] // 8 is the kind and param_target[p] % 8 the zone of parameter p.
All inputs are finite; a program needn't handle non-finite values.
Results may differ from a plain program's by a relative error of at most 0.0003.
Values sent between devices are 32-bit elements; how exact they have to be, the bound alone decides.
A program may use at most 128 MiB of HBM per device.

v0:
```python
import jax
import jax.numpy as jnp
from jax import lax
from jax.sharding import PartitionSpec as P

STEP_LENGTH = 0.15
AXIAL_MIX = 0.5
RADIAL_MIX = 0.25
VELOCITY = 1.0
FILM_SCALE = 1.5
SHELL_WEIGHTS = (0.3, 0.6, 0.9, 1.2, 1.5)


def padded_2(shard, sides, width):
    for axis, dim in sides:
        count, length = (lax.axis_size(axis), shard.shape[dim])
        up = [(i, (i + 1) % count) for i in range(count - 1)]
        down = [(j, i) for i, j in up]
        last = lax.slice_in_dim(shard, length - width, length, axis=dim)
        first = lax.slice_in_dim(shard, 0, width, axis=dim)
        before = lax.ppermute(last, axis, up)
        after = lax.ppermute(first, axis, down)
        shard = jnp.concatenate([before, shard, after], axis=dim)
    return shard


def field_slice(values, lower_end, upper_end):
    return values[..., lower_end:upper_end, :, :, :]


def transport(padded):
    center = padded[..., 1:-1, 1:-1, :]
    widths = [(0, 0)] * (center.ndim - 1) + [(1, 1)]
    column = jnp.pad(center, widths)
    behind = padded[..., :-2, 1:-1, :]
    ahead = padded[..., 2:, 1:-1, :]
    lower_row = padded[..., 1:-1, :-2, :]
    upper_row = padded[..., 1:-1, 2:, :]
    axial = AXIAL_MIX * (ahead + behind - 2.0 * center)
    radial = RADIAL_MIX * (
        lower_row + upper_row + column[..., 2:] + column[..., :-2] - 4.0 * center
    )
    return axial + radial - VELOCITY * (center - behind)


def bulk_rate(padded, outer_shell, film_rate, packing):
    center = padded[..., 1:-1, 1:-1, :]
    return transport(padded) - film_rate * packing * (center - outer_shell)


def bulk_tangent(
    tangent_padded, tangent_outer, tangent_film, bulk_conc, outer_shell, film_rate, packing
):
    tangent_center = tangent_padded[..., 1:-1, 1:-1, :]
    return transport(tangent_padded) - (
        tangent_film * packing * (bulk_conc - outer_shell)
        + film_rate * packing * (tangent_center - tangent_outer)
    )


def shell_flux(shells):
    fluxes = [
        SHELL_WEIGHTS[shell_index]
        * (
            field_slice(shells, shell_index + 1, shell_index + 2)
            - field_slice(shells, shell_index, shell_index + 1)
        )
        for shell_index in range(5)
    ]
    shell_rows = (
        [fluxes[0]]
        + [fluxes[shell_index] - fluxes[shell_index - 1] for shell_index in range(1, 5)]
        + [-fluxes[4]]
    )
    return jnp.concatenate(shell_rows, axis=-4)


def pellet_rate(bulk_conc, pore_one, pore_two, theta_field):
    denominator = (
        1.0 + field_slice(theta_field, 6, 7) * pore_one + field_slice(theta_field, 7, 8) * pore_two
    )
    result_parts = []
    for component, pore_conc in ((0, pore_one), (1, pore_two)):
        film_rate = field_slice(theta_field, component, component + 1)
        diffusion = field_slice(theta_field, 2 + component, 3 + component)
        capacity = field_slice(theta_field, 4 + component, 5 + component)
        affinity = field_slice(theta_field, 6 + component, 7 + component)
        change = diffusion * shell_flux(pore_conc) - capacity * affinity * pore_conc / denominator
        surface = (
            FILM_SCALE
            * film_rate
            * (field_slice(bulk_conc, component, component + 1) - field_slice(pore_conc, 5, 6))
        )
        result_parts.append(field_slice(change, 0, 5))
        result_parts.append(field_slice(change, 5, 6) + surface)
    return jnp.concatenate(result_parts, axis=-4)


def pellet_tangent(
    bulk_conc,
    pore_one,
    pore_two,
    theta_field,
    tangent_bulk,
    tangent_one,
    tangent_two,
    tangent_theta,
):
    denominator = (
        1.0 + field_slice(theta_field, 6, 7) * pore_one + field_slice(theta_field, 7, 8) * pore_two
    )
    tangent_denominator = (
        field_slice(theta_field, 6, 7) * tangent_one
        + pore_one * field_slice(tangent_theta, 6, 7)
        + field_slice(theta_field, 7, 8) * tangent_two
        + pore_two * field_slice(tangent_theta, 7, 8)
    )
    result_parts = []
    for component, pore_conc, tangent_pore in (
        (0, pore_one, tangent_one),
        (1, pore_two, tangent_two),
    ):
        film_rate = field_slice(theta_field, component, component + 1)
        diffusion = field_slice(theta_field, 2 + component, 3 + component)
        capacity = field_slice(theta_field, 4 + component, 5 + component)
        affinity = field_slice(theta_field, 6 + component, 7 + component)
        tangent_film = field_slice(tangent_theta, component, component + 1)
        tangent_diffusion = field_slice(tangent_theta, 2 + component, 3 + component)
        tangent_capacity = field_slice(tangent_theta, 4 + component, 5 + component)
        tangent_affinity = field_slice(tangent_theta, 6 + component, 7 + component)
        uptake_tangent = (
            tangent_capacity * affinity * pore_conc
            + capacity * tangent_affinity * pore_conc
            + capacity * affinity * tangent_pore
        ) / denominator - capacity * affinity * pore_conc * tangent_denominator / (
            denominator * denominator
        )
        change = (
            tangent_diffusion * shell_flux(pore_conc)
            + diffusion * shell_flux(tangent_pore)
            - uptake_tangent
        )
        surface = FILM_SCALE * (
            tangent_film
            * (field_slice(bulk_conc, component, component + 1) - field_slice(pore_conc, 5, 6))
            + film_rate
            * (
                field_slice(tangent_bulk, component, component + 1)
                - field_slice(tangent_pore, 5, 6)
            )
        )
        result_parts.append(field_slice(change, 0, 5))
        result_parts.append(field_slice(change, 5, 6) + surface)
    return jnp.concatenate(result_parts, axis=-4)


def zone_lookup(table, zones):
    result = jnp.zeros((table.shape[0],) + zones.shape, table.dtype)
    for zone_index in range(table.shape[1]):
        result = jnp.where(
            zones[None] == zone_index, table[:, zone_index][:, None, None, None], result
        )
    return result


def zone_tangents(targets, zones, kind_count, zone_count):
    kind_of = targets // zone_count
    zone_of = targets % zone_count
    chosen = (kind_of[:, None] == jnp.arange(kind_count)[None, :]).astype(jnp.float32)
    within = (zones[None] == zone_of[:, None, None, None]).astype(jnp.float32)
    return chosen[:, :, None, None, None] * within[:, None]


def outer_shells(values):
    return jnp.concatenate([field_slice(values, 7, 8), field_slice(values, 13, 14)], axis=-4)


def advance_state(padded, state_now, theta_field, packing):
    bulk_conc = field_slice(state_now, 0, 2)
    new_bulk = bulk_conc + STEP_LENGTH * bulk_rate(
        padded, outer_shells(state_now), field_slice(theta_field, 0, 2), packing
    )
    new_pores = field_slice(state_now, 2, 14) + STEP_LENGTH * pellet_rate(
        bulk_conc, field_slice(state_now, 2, 8), field_slice(state_now, 8, 14), theta_field
    )
    return jnp.concatenate([new_bulk, new_pores], axis=-4)


def advance_tangent(tangent_padded, tangent_now, state_now, theta_field, tangent_theta, packing):
    bulk_conc = field_slice(state_now, 0, 2)
    new_bulk = field_slice(tangent_now, 0, 2) + STEP_LENGTH * bulk_tangent(
        tangent_padded,
        outer_shells(tangent_now),
        field_slice(tangent_theta, 0, 2),
        bulk_conc,
        outer_shells(state_now),
        field_slice(theta_field, 0, 2),
        packing,
    )
    new_pores = field_slice(tangent_now, 2, 14) + STEP_LENGTH * pellet_tangent(
        bulk_conc,
        field_slice(state_now, 2, 8),
        field_slice(state_now, 8, 14),
        theta_field,
        field_slice(tangent_now, 0, 2),
        field_slice(tangent_now, 2, 8),
        field_slice(tangent_now, 8, 14),
        tangent_theta,
    )
    return jnp.concatenate([new_bulk, new_pores], axis=-4)


def shards(state, sensitivity, packing, cell_zone, coefficients, param_target):
    column_width = state.shape[3]
    kind_count = coefficients.shape[0]
    zone_count = coefficients.shape[1]
    current = lax.all_gather(state, "param", axis=3, tiled=True)
    theta_field = zone_lookup(coefficients, cell_zone)
    tangent_theta = zone_tangents(param_target, cell_zone, kind_count, zone_count)
    tangent_now = sensitivity
    for time_index in range(2):
        stacked = jnp.concatenate([field_slice(current, 0, 2)[None], tangent_now[:, 0:2]], axis=0)
        padded_all = padded_2(stacked, (("slab", 2), ("tile", 3)), 1)
        padded = padded_all[0]
        tangent_padded = padded_all[1:]
        tangent_now = advance_tangent(
            tangent_padded, tangent_now, current, theta_field, tangent_theta, packing
        )
        current = advance_state(padded, current, theta_field, packing)
    column_start = lax.axis_index("param") * column_width
    final_state = lax.dynamic_slice_in_dim(current, column_start, column_width, 3)
    return (final_state, tangent_now)


def solution(mesh):
    placed = (
        P(None, "slab", "tile", "param"),
        P("param", None, "slab", "tile", None),
        P("slab", "tile", None),
        P("slab", "tile", None),
        P(),
        P("param"),
    )
    return jax.shard_map(
        shards,
        mesh=mesh,
        in_specs=placed,
        out_specs=(P(None, "slab", "tile", "param"), P("param", None, "slab", "tile", None)),
        check_vma=False,
    )
```

profile of v0, /device:TPU:26, one launch (start us, length us, event | category | flops | bytes accessed | tf_op | source)
XLA Modules:
  0.0 164.6 jit_solution(4070820556572773379)
XLA Ops:
  0.6 1.2 slice.685
  1.8 32.7 %all_gather.3 = f32[14,3,32,128]{2,3,1,0:T(8,128)S(1)} all-gather(f32[14,3,32,16]{2,3,1,0:T(8,128)} %param.6), channel_id=1, replica_groups=mesh['param'=8,'slab'=8,'tile'=4] {'param'}, dimensions={3}, use_global_device_ids=true | all-gather | bytes 774144 | tf_op jit(solution)/shard_map/all_gather | solution.py:217
  35.3 1.8 %copy.241 = f32[2,3,32,128]{3,2,1,0:T(8,128)} copy(f32[2,3,32,128]{2,3,1,0:T(8,128)} %slice.830) | data formatting | bytes 196608
  37.1 1.7 %pad_maximum_fusion.28 = (f32[9,2,1,32,128]{4,3,2,1,0:T(8,128)}, f32[9,2,1,32,128]{4,3,2,1,0:T(8,128)}) fusion(f32[8,2,3,32,128]{4,3,2,1,0:T(8,128)S(1)} %slice.685, f32[1,2,3,32,128]{4,3,2,1,0:T(8,128)} %bitcast.54), kind=kLoop, calls=%fused_computation.159 | loop fusion | flops 147456 | bytes 1474560 | tf_op jit(solution)/shard_map/slice | solution.py:19
  38.8 3.2 %collective-permute-start = (f32[9,2,1,32,128]{4,3,2,1,0:T(8,128)}, f32[9,2,1,32,128]{4,3,2,1,0:T(8,128)}, u32[]{:S(2)}, u32[]{:S(2)}) collective-permute-start(f32[9,2,1,32,128]{4,3,2,1,0:T(8,128)} %get-tuple-element.91), channel_id=1, source_target_pairs={{0,4},{4,8},{8,12},{12,16},{16,20},{20,24},{24,28},{1,5},{5,9},{9,... | collective-permute-start | bytes 884744 | tf_op jit(solution)/shard_map/ppermute | solution.py:21
  42.0 3.6 %collective-permute-start.1 = (f32[9,2,1,32,128]{4,3,2,1,0:T(8,128)}, f32[9,2,1,32,128]{4,3,2,1,0:T(8,128)}, u32[]{:S(2)}, u32[]{:S(2)}) collective-permute-start(f32[9,2,1,32,128]{4,3,2,1,0:T(8,128)} %get-tuple-element.92), channel_id=1, source_target_pairs={{4,0},{8,4},{12,8},{16,12},{20,16},{24,20},{28,24},{5,1},{9,5},{13... | collective-permute-start | bytes 884744 | tf_op jit(solution)/shard_map/ppermute | solution.py:22
  45.5 1.9 %fusion.62 = f32[8,6,3,32,128]{4,3,2,1,0:T(8,128)} fusion(f32[8,14,3,32,128]{4,3,2,1,0:T(8,128)} %param.7), kind=kLoop, calls=%fused_computation.186 | loop fusion | flops 196607 | bytes 1179648
  47.5 1.6 slice.845
  49.0 1.6 fusion.100
  50.6 1.5 fusion.99
  53.7 3.2 %copy.248 = f32[12,3,32,128]{3,2,1,0:T(8,128)} copy(f32[12,3,32,128]{2,3,1,0:T(8,128)} %slice.845) | data formatting | bytes 1179648
  56.9 1.7 %copy.254 = f32[6,3,32,128]{3,2,1,0:T(8,128)S(1)} copy(f32[6,3,32,128]{2,3,1,0:T(8,128)} %get-tuple-element.79) | data formatting | bytes 589824
  59.4 1.0 copy.245
  60.4 1.1 copy.244
  61.4 1.7 %copy.261 = f32[1,3,32,128]{3,2,1,0:T(8,128)} copy(f32[1,3,32,128]{2,3,1,0:T(8,128)} %get-tuple-element.66) | data formatting | bytes 98304
  63.1 1.6 %copy.260 = f32[1,3,32,128]{3,2,1,0:T(8,128)} copy(f32[1,3,32,128]{2,3,1,0:T(8,128)} %get-tuple-element.67) | data formatting | bytes 98304
  64.8 1.6 copy.259
  66.4 1.6 %copy.257 = f32[1,3,32,128]{3,2,1,0:T(8,128)} copy(f32[1,3,32,128]{2,3,1,0:T(8,128)} %get-tuple-element.70) | data formatting | bytes 98304
  68.1 1.6 copy.253
  69.7 1.6 %copy.252 = f32[1,3,32,128]{3,2,1,0:T(8,128)} copy(f32[1,3,32,128]{2,3,1,0:T(8,128)} %get-tuple-element.72) | data formatting | bytes 98304
  71.3 1.6 copy.251
  73.0 1.7 %copy.249 = f32[1,3,32,128]{3,2,1,0:T(8,128)} copy(f32[1,3,32,128]{2,3,1,0:T(8,128)} %get-tuple-element.75) | data formatting | bytes 98304
  74.6 1.6 %copy.258 = f32[1,3,32,128]{3,2,1,0:T(8,128)} copy(f32[1,3,32,128]{2,3,1,0:T(8,128)} %get-tuple-element.69) | data formatting | bytes 98304
  78.1 0.8 constant_dynamic-update-slice_fusion.5
  78.9 0.9 constant_dynamic-update-slice_fusion.4
  79.8 0.9 constant_dynamic-update-slice_fusion.3
  80.7 1.0 constant_dynamic-update-slice_fusion.2
  81.7 1.1 constant_dynamic-update-slice_fusion.1
  82.9 0.8 constant_dynamic-update-slice_fusion.9
  83.7 0.8 constant_dynamic-update-slice_fusion.8
  84.5 0.8 constant_dynamic-update-slice_fusion.7
  85.4 0.8 constant_dynamic-update-slice_fusion
  87.1 1.0 divide_subtract_fusion.3
  91.6 2.1 %broadcast_multiply_fusion = f32[8,8,3,32,128]{4,3,2,1,0:T(8,128)} fusion(f32[8,3,32,128]{3,2,1,0:T(8,128)S(1)} %compare_convert_fusion, f32[8,8]{1,0:T(8,128)S(1)} %fusion.94), kind=kLoop, calls=%fused_computation.27 | loop fusion | flops 786432 | bytes 3539200 | tf_op jit(solution)/shard_map/mul | solution.py:171
  94.4 1.3 divide_subtract_fusion.1
  95.7 1.1 pad_maximum_fusion.48
  98.0 3.3 %collective-permute-start.3 = (f32[9,2,5,1,128]{4,1,3,2,0:T(2,128)}, f32[9,2,5,1,128]{4,1,3,2,0:T(2,128)}, u32[]{:S(2)}, u32[]{:S(2)}) collective-permute-start(f32[9,2,5,1,128]{4,1,3,2,0:T(2,128)} %copy.243), channel_id=1, source_target_pairs={{1,0},{2,1},{3,2},{5,4},{6,5},{7,6},{9,8},{10,9},{11,10},{13,12},{... | collective-permute-start | bytes 138248 | tf_op jit(solution)/shard_map/ppermute | solution.py:22
  101.3 1.3 collective-permute-start.2
  102.7 1.4 copy-done.15
  104.1 1.7 %slice.881 = f32[5,3,32,128]{3,2,1,0:T(8,128)} slice(f32[6,3,32,128]{3,2,1,0:T(8,128)} %get-tuple-element.27), slice={[0:5], [0:3], [0:32], [0:128]} | slice | bytes 491520 | tf_op jit(solution)/shard_map/slice | solution.py:28
  105.8 1.7 %slice.889 = f32[5,3,32,128]{3,2,1,0:T(8,128)} slice(f32[6,3,32,128]{3,2,1,0:T(8,128)} %get-tuple-element.89), slice={[0:5], [0:3], [0:32], [0:128]} | slice | bytes 491520 | tf_op jit(solution)/shard_map/slice | solution.py:28
  107.4 1.0 copy.214
  108.4 0.8 copy.213
  109.3 1.0 fusion.61
  110.3 2.0 %fusion.88 = (f32[2,3,32,128]{3,2,1,0:T(8,128)}, f32[2,3,32,128]{3,2,1,0:T(8,128)S(1)}, f32[2,3,32,128]{3,2,1,0:T(8,128)S(1)}, f32[2,3,32,128]{3,2,1,0:T(8,128)S(1)}) fusion(f32[1,3,32,128]{3,2,1,0:T(8,128)} %get-tuple-element.101, f32[1,3,32,128]{3,2,1,0:T(8,128)} %get-tuple-element.102, f32[2,3,32,128]{3,2,1,0:T(8,128)S(1)} %copy-done.10, ...), kind=kLoop, calls=%fused_computation.243 | loop fusion | flops 565248 | bytes 1327104 | tf_op jit(solution)/shard_map/sub | solution.py:56
  112.3 1.0 fusion.92
  114.6 3.0 %fusion.10 = f32[8,6,3,32,128]{4,3,2,1,0:T(8,128)S(1)} fusion(f32[8,6,3,32,128]{4,3,2,1,0:T(8,128)} %copy-done.15, f32[8,14,3,32,128]{4,3,2,1,0:T(8,128)S(1)} %bitcast.49, f32[8,3,32,128]{3,2,1,0:T(8,128)S(1)} %get-tuple-element.60, f32[6,3,32,128]{3,2,1,0:T(8,128)S(1)} %copy-done.53, f32[3,32,128]{2,1,0:T(8,128)S(1)} %copy-done.44, ...), kind=kLoop, calls=%fused_computation.16 | loop fusion | flops 10616832 | bytes 12976128 | tf_op jit(solution)/shard_map/sub | solution.py:139
  117.7 2.5 %copy-done.14 = f32[8,6,3,32,128]{4,3,2,1,0:T(8,128)S(1)} copy-done((f32[8,6,3,32,128]{4,3,2,1,0:T(8,128)S(1)}, f32[8,6,3,32,128]{4,3,2,1,0:T(8,128)}, u32[]{:S(2)}) %copy-start.14) | copy-done | bytes 2359320
  120.3 1.7 %fusion.13 = f32[8,6,3,32,128]{4,3,2,1,0:T(8,128)S(1)} fusion(f32[8,6,3,32,128]{4,3,2,1,0:T(8,128)S(1)} %copy-done.14, f32[8,14,3,32,128]{4,3,2,1,0:T(8,128)S(1)} %bitcast.49, f32[8,3,32,128]{3,2,1,0:T(8,128)S(1)} %get-tuple-element.64, f32[6,3,32,128]{3,2,1,0:T(8,128)S(1)} %copy-done.21, f32[6,3,32,128]{3,2,1,0:T(8,128)S(1)} %copy-done.51, ...), kind=kLoop, calls=%fused_computation.20 | loop fusion | flops 10616832 | bytes 12976128 | tf_op jit(solution)/shard_map/sub | solution.py:139
  122.0 0.8 copy-done.68
  123.8 2.0 %fusion.22 = f32[8,2,3,32,128]{4,3,2,1,0:T(8,128)S(1)} fusion(f32[8,2,3,32,128]{4,3,2,1,0:T(8,128)S(1)} %slice.685, f32[9,2,5,1,128]{4,3,2,1,0:T(1,128)S(1)} %copy.214, f32[9,2,1,32,128]{4,3,2,1,0:T(8,128)} %collective-permute-done.1, f32[9,2,1,32,128]{4,3,2,1,0:T(8,128)} %collective-permute-done, f32[1,2,3,32,128]{4,3,2,1,0:T(8,128)S(1)} %bitcast.57, ...), kind=kLoop, calls=%fused_computation.36 | loop fusion | flops 6684672 | bytes 4171776 | tf_op jit(solution)/shard_map/add | solution.py:191
  125.9 2.3 %collective-permute-start.4 = (f32[9,2,1,32,128]{4,3,2,1,0:T(8,128)S(1)}, f32[9,2,1,32,128]{4,3,2,1,0:T(8,128)S(1)}, u32[]{:S(2)}, u32[]{:S(2)}) collective-permute-start(f32[9,2,1,32,128]{4,3,2,1,0:T(8,128)S(1)} %get-tuple-element.87), channel_id=1, source_target_pairs={{0,4},{4,8},{8,12},{12,16},{16,20},{20,24},{24,28},{1,5},{5,9},{9,... | collective-permute-start | bytes 884744 | tf_op jit(solution)/shard_map/ppermute | solution.py:21
  128.2 4.6 %collective-permute-start.5 = (f32[9,2,1,32,128]{4,3,2,1,0:T(8,128)S(1)}, f32[9,2,1,32,128]{4,3,2,1,0:T(8,128)S(1)}, u32[]{:S(2)}, u32[]{:S(2)}) collective-permute-start(f32[9,2,1,32,128]{4,3,2,1,0:T(8,128)S(1)} %get-tuple-element.88), channel_id=1, source_target_pairs={{4,0},{8,4},{12,8},{16,12},{20,16},{24,20},{28,24},{5,1},{9,5},{13... | collective-permute-start | bytes 884744 | tf_op jit(solution)/shard_map/ppermute | solution.py:22
  132.9 1.3 fusion
  135.4 0.9 fusion.98
  136.8 1.7 %fusion.4 = f32[8,6,3,32,128]{4,3,2,1,0:T(8,128)S(1)} fusion(f32[8,6,3,32,128]{4,3,2,1,0:T(8,128)S(1)} %get-tuple-element.50, f32[8,12,3,32,128]{4,3,2,1,0:T(8,128)S(1)} %fusion, f32[8,3,32,128]{3,2,1,0:T(8,128)S(1)} %get-tuple-element.60, f32[6,3,32,128]{3,2,1,0:T(8,128)S(1)} %copy-done.54, f32[6,3,32,128]{3,2,1,0:T(8,128)S(1)} %copy-done.35, ...), kind=kLoop, calls=%fused_computation.8 | loop fusion | flops 10616832 | bytes 12976128 | tf_op jit(solution)/shard_map/sub | solution.py:139
  139.6 1.7 %fusion.7 = f32[8,6,3,32,128]{4,3,2,1,0:T(8,128)S(1)} fusion(f32[8,6,3,32,128]{4,3,2,1,0:T(8,128)S(1)} %get-tuple-element.51, f32[8,12,3,32,128]{4,3,2,1,0:T(8,128)S(1)} %fusion, f32[8,3,32,128]{3,2,1,0:T(8,128)S(1)} %get-tuple-element.64, f32[6,3,32,128]{3,2,1,0:T(8,128)S(1)} %copy-done.20, f32[6,3,32,128]{3,2,1,0:T(8,128)S(1)} %copy-done.52, ...), kind=kLoop, calls=%fused_computation.12 | loop fusion | flops 10616832 | bytes 12976128 | tf_op jit(solution)/shard_map/sub | solution.py:139
  142.0 2.8 %fusion.1 = f32[8,12,3,32,128]{4,3,2,1,0:T(8,128)} fusion(f32[8,12,3,32,128]{4,3,2,1,0:T(8,128)S(1)} %fusion, f32[8,1,3,32,128]{4,3,2,1,0:T(8,128)S(1)} %get-tuple-element.36, f32[8,5,3,32,128]{4,3,2,1,0:T(8,128)S(1)} %slice.921, f32[8,1,3,32,128]{4,3,2,1,0:T(8,128)S(1)} %get-tuple-element.35, f32[8,5,3,32,128]{4,3,2,1,0:T(8,128)S(1)} %slice.913), kind=kLoop, calls=%fused_computation.4 | loop fusion | flops 5898240 | bytes 14155776 | tf_op jit(solution)/shard_map/add | solution.py:200
  145.0 4.5 %collective-permute-start.7 = (f32[9,2,5,1,128]{4,1,3,2,0:T(2,128)S(1)}, f32[9,2,5,1,128]{4,1,3,2,0:T(2,128)S(1)}, u32[]{:S(2)}, u32[]{:S(2)}) collective-permute-start(f32[9,2,5,1,128]{4,1,3,2,0:T(2,128)S(1)} %copy.247), channel_id=1, source_target_pairs={{1,0},{2,1},{3,2},{5,4},{6,5},{7,6},{9,8},{10,9},{11,10},{13,12},{... | collective-permute-start | bytes 138248 | tf_op jit(solution)/shard_map/ppermute | solution.py:22
  149.5 1.3 collective-permute-start.6
  151.3 4.2 %collective-permute-done.6 = f32[9,2,5,1,128]{4,1,3,2,0:T(2,128)S(1)} collective-permute-done((f32[9,2,5,1,128]{4,1,3,2,0:T(2,128)S(1)}, f32[9,2,5,1,128]{4,1,3,2,0:T(2,128)S(1)}, u32[]{:S(2)}, u32[]{:S(2)}) %collective-permute-start.6) | collective-permute-done | bytes 46112 | tf_op jit(solution)/shard_map/ppermute | solution.py:21
  156.0 1.0 copy.240
  157.0 2.0 %fusion.31 = f32[8,2,3,32,128]{4,3,2,1,0:T(8,128)S(1)} fusion(f32[8,2,3,32,128]{4,3,2,1,0:T(8,128)S(1)} %fusion.22, f32[9,2,5,1,128]{4,3,2,1,0:T(1,128)S(1)} %copy.222, f32[9,2,1,32,128]{4,3,2,1,0:T(8,128)S(1)} %collective-permute-done.5, f32[9,2,1,32,128]{4,3,2,1,0:T(8,128)S(1)} %collective-permute-done.4, f32[1,2,3,32,128]{4,3,2,1,0:T(8,128)S(1)} %bitcast.53, ...), kind=kLoop, calls=%fused_computation.45 | loop fusion | flops 6684672 | bytes 4171776 | tf_op jit(solution)/shard_map/add | solution.py:191
  159.0 5.6 %pad_maximum_fusion = f32[8,14,3,32,128]{4,3,2,1,0:T(8,128)} fusion(f32[8,12,3,32,128]{4,3,2,1,0:T(8,128)} %fusion.1, f32[8,2,3,32,128]{4,3,2,1,0:T(8,128)S(1)} %fusion.31), kind=kLoop, calls=%fused_computation | loop fusion | flops 1376256 | bytes 11010048 | tf_op jit(solution)/shard_map/concatenate | solution.py:210
  (229 shorter events, 17.6 us)
Async XLA Ops:
  38.8 56.9 %collective-permute-start = (f32[9,2,1,32,128]{4,3,2,1,0:T(8,128)}, f32[9,2,1,32,128]{4,3,2,1,0:T(8,128)}, u32[]{:S(2)}, u32[]{:S(2)}) collective-permute-start(f32[9,2,1,32,128]{4,3,2,1,0:T(8,128)} %get-tuple-element.91), channel_id=1, source_target_pairs={{0,4},{4,8},{8,12},{12,16},{16,20},{20,24},{24,28},{1,5},{5,9},{9,... | collective-permute-start | bytes 884744 | tf_op jit(solution)/shard_map/ppermute | solution.py:21
  42.0 53.7 %collective-permute-start.1 = (f32[9,2,1,32,128]{4,3,2,1,0:T(8,128)}, f32[9,2,1,32,128]{4,3,2,1,0:T(8,128)}, u32[]{:S(2)}, u32[]{:S(2)}) collective-permute-start(f32[9,2,1,32,128]{4,3,2,1,0:T(8,128)} %get-tuple-element.92), channel_id=1, source_target_pairs={{4,0},{8,4},{12,8},{16,12},{20,16},{24,20},{28,24},{5,1},{9,5},{13... | collective-permute-start | bytes 884744 | tf_op jit(solution)/shard_map/ppermute | solution.py:22
  50.6 1.5 copy-start.67
  50.6 1.8 %copy-start.72 = (s32[3,32,128]{2,1,0:T(8,128)S(1)}, s32[3,32,128]{2,1,0:T(8,128)}, u32[]{:S(2)}) copy-start(s32[3,32,128]{2,1,0:T(8,128)} %param.9) | copy-start | bytes 147460
  52.9 35.3 %copy-start.19 = (f32[8,3,32,128]{3,2,1,0:T(8,128)}, f32[8,3,32,128]{3,2,1,0:T(8,128)S(1)}, u32[]{:S(2)}) copy-start(f32[8,3,32,128]{3,2,1,0:T(8,128)S(1)} %select_select_fusion) | copy-start | bytes 1179652
  53.6 33.4 %copy-start.36 = (f32[3,32,128]{2,1,0:T(8,128)}, f32[3,32,128]{2,1,0:T(8,128)S(1)}, u32[]{:S(2)}) copy-start(f32[3,32,128]{2,1,0:T(8,128)S(1)} %get-tuple-element.115) | copy-start | bytes 147460
  53.6 33.4 %copy-start.39 = (f32[3,32,128]{2,1,0:T(8,128)}, f32[3,32,128]{2,1,0:T(8,128)S(1)}, u32[]{:S(2)}) copy-start(f32[3,32,128]{2,1,0:T(8,128)S(1)} %get-tuple-element.120) | copy-start | bytes 147460
  53.6 33.4 %copy-start.42 = (f32[3,32,128]{2,1,0:T(8,128)}, f32[3,32,128]{2,1,0:T(8,128)S(1)}, u32[]{:S(2)}) copy-start(f32[3,32,128]{2,1,0:T(8,128)S(1)} %get-tuple-element.117) | copy-start | bytes 147460
  53.6 35.4 %copy-start.16 = (f32[3,32,128]{2,1,0:T(8,128)}, f32[3,32,128]{2,1,0:T(8,128)S(1)}, u32[]{:S(2)}) copy-start(f32[3,32,128]{2,1,0:T(8,128)S(1)} %get-tuple-element.119) | copy-start | bytes 147460
  53.6 5.0 %copy-start.59 = (f32[1,3,32,128]{2,3,1,0:T(8,128)S(1)}, f32[1,3,32,128]{2,3,1,0:T(8,128)}, u32[]{:S(2)}) copy-start(f32[1,3,32,128]{2,3,1,0:T(8,128)} %get-tuple-element.65) | copy-start | bytes 147460
  56.9 19.4 %copy-start.58 = (f32[1,3,32,128]{2,3,1,0:T(8,128)S(1)}, f32[1,3,32,128]{2,3,1,0:T(8,128)}, u32[]{:S(2)}) copy-start(f32[1,3,32,128]{2,3,1,0:T(8,128)} %get-tuple-element.74) | copy-start | bytes 147460
  56.9 20.1 %copy-start.57 = (f32[1,3,32,128]{2,3,1,0:T(8,128)S(1)}, f32[1,3,32,128]{2,3,1,0:T(8,128)}, u32[]{:S(2)}) copy-start(f32[1,3,32,128]{2,3,1,0:T(8,128)} %get-tuple-element.78) | copy-start | bytes 147460
  56.9 20.9 %copy-start.9 = (f32[6,3,32,128]{2,3,1,0:T(8,128)S(1)}, f32[6,3,32,128]{2,3,1,0:T(8,128)}, u32[]{:S(2)}) copy-start(f32[6,3,32,128]{2,3,1,0:T(8,128)} %get-tuple-element.80) | copy-start | bytes 884740
  60.4 25.0 %copy-start.47 = (f32[1,3,32,128]{3,2,1,0:T(8,128)}, f32[1,3,32,128]{3,2,1,0:T(8,128)S(1)}, u32[]{:S(2)}) copy-start(f32[1,3,32,128]{3,2,1,0:T(8,128)S(1)} %copy.245) | copy-start | bytes 147460
  61.4 23.9 %copy-start.49 = (f32[1,3,32,128]{3,2,1,0:T(8,128)}, f32[1,3,32,128]{3,2,1,0:T(8,128)S(1)}, u32[]{:S(2)}) copy-start(f32[1,3,32,128]{3,2,1,0:T(8,128)S(1)} %copy.244) | copy-start | bytes 147460
  77.7 5.0 %copy-start.61 = (f32[1,3,32,128]{3,2,1,0:T(8,128)S(1)}, f32[1,3,32,128]{3,2,1,0:T(8,128)}, u32[]{:S(2)}) copy-start(f32[1,3,32,128]{3,2,1,0:T(8,128)} %copy.257) | copy-start | bytes 147460
  77.7 5.1 %copy-start.64 = (f32[1,3,32,128]{3,2,1,0:T(8,128)S(1)}, f32[1,3,32,128]{3,2,1,0:T(8,128)}, u32[]{:S(2)}) copy-start(f32[1,3,32,128]{3,2,1,0:T(8,128)} %copy.258) | copy-start | bytes 147460
  77.7 5.1 %copy-start.60 = (f32[1,3,32,128]{3,2,1,0:T(8,128)S(1)}, f32[1,3,32,128]{3,2,1,0:T(8,128)}, u32[]{:S(2)}) copy-start(f32[1,3,32,128]{3,2,1,0:T(8,128)} %copy.259) | copy-start | bytes 147460
  78.1 9.0 %copy-start.45 = (f32[3,32,128]{2,1,0:T(8,128)S(1)}, f32[3,32,128]{2,1,0:T(8,128)}, u32[]{:S(2)}) copy-start(f32[3,32,128]{2,1,0:T(8,128)} %get-tuple-element.118) | copy-start | bytes 147460
  80.7 9.4 %slice-start = ((s8[5505024]{0:T(1024)(128)(4,1)}), s8[4194304]{0:T(1024)(128)(4,1)S(1)}, s32[]{:S(2)}) async-start(s8[5505024]{0:T(1024)(128)(4,1)} %bitcast.46), calls=%async_computation | async-start | bytes 8388608
  86.2 2.0 %copy-start.30 = (f32[6,3,32,128]{3,2,1,0:T(8,128)}, f32[6,3,32,128]{3,2,1,0:T(8,128)S(1)}, u32[]{:S(2)}) copy-start(f32[6,3,32,128]{3,2,1,0:T(8,128)S(1)} %get-tuple-element.136) | copy-start | bytes 884740
  86.2 2.0 %copy-start.32 = (f32[6,3,32,128]{3,2,1,0:T(8,128)}, f32[6,3,32,128]{3,2,1,0:T(8,128)S(1)}, u32[]{:S(2)}) copy-start(f32[6,3,32,128]{3,2,1,0:T(8,128)S(1)} %get-tuple-element.137) | copy-start | bytes 884740
  86.2 2.0 %copy-start.48 = (f32[1,3,32,128]{3,2,1,0:T(8,128)S(1)}, f32[1,3,32,128]{3,2,1,0:T(8,128)}, u32[]{:S(2)}) copy-start(f32[1,3,32,128]{3,2,1,0:T(8,128)} %copy-done.47) | copy-start | bytes 147460
  86.2 2.0 %copy-start.50 = (f32[1,3,32,128]{3,2,1,0:T(8,128)S(1)}, f32[1,3,32,128]{3,2,1,0:T(8,128)}, u32[]{:S(2)}) copy-start(f32[1,3,32,128]{3,2,1,0:T(8,128)} %copy-done.49) | copy-start | bytes 147460
  86.3 2.0 %copy-start.70 = (f32[1,3,32,128]{3,2,1,0:T(8,128)S(1)}, f32[1,3,32,128]{3,2,1,0:T(8,128)}, u32[]{:S(2)}) copy-start(f32[1,3,32,128]{3,2,1,0:T(8,128)} %copy.256) | copy-start | bytes 147460
  86.3 2.0 %copy-start.71 = (f32[1,3,32,128]{3,2,1,0:T(8,128)S(1)}, f32[1,3,32,128]{3,2,1,0:T(8,128)}, u32[]{:S(2)}) copy-start(f32[1,3,32,128]{3,2,1,0:T(8,128)} %copy.262) | copy-start | bytes 147460
  87.1 1.8 %copy-start.7 = (f32[6,3,32,128]{3,2,1,0:T(8,128)}, f32[6,3,32,128]{3,2,1,0:T(8,128)S(1)}, u32[]{:S(2)}) copy-start(f32[6,3,32,128]{3,2,1,0:T(8,128)S(1)} %get-tuple-element.26) | copy-start | bytes 884740
  87.1 1.8 %copy-start.24 = (f32[12,3,32,128]{3,2,1,0:T(8,128)S(1)}, f32[12,3,32,128]{3,2,1,0:T(8,128)}, u32[]{:S(2)}) copy-start(f32[12,3,32,128]{3,2,1,0:T(8,128)} %copy.248) | copy-start | bytes 1769476
  87.1 3.0 %slice-start.1 = ((s8[5505024]{0:T(1024)(128)(4,1)}), s8[1310720]{0:T(1024)(128)(4,1)S(1)}, s32[]{:S(2)}) async-start(s8[5505024]{0:T(1024)(128)(4,1)} %bitcast.46), calls=%async_computation.1 | async-start | bytes 2621440
  88.1 1.8 %copy-start.74 = (s32[8]{0:T(128)S(1)}, s32[8]{0:T(128)}, u32[]{:S(2)}) copy-start(s32[8]{0:T(128)} %param.11) | copy-start | bytes 100
  88.1 1.8 %copy-start.73 = (s32[3,32,128]{2,1,0:T(8,128)S(1)}, s32[3,32,128]{2,1,0:T(8,128)}, u32[]{:S(2)}) copy-start(s32[3,32,128]{2,1,0:T(8,128)} %param.9) | copy-start | bytes 147460
  88.1 1.9 %copy-start.12 = (f32[8,6,3,32,128]{4,3,2,1,0:T(8,128)S(1)}, f32[8,6,3,32,128]{4,3,2,1,0:T(8,128)}, u32[]{:S(2)}) copy-start(f32[8,6,3,32,128]{4,3,2,1,0:T(8,128)} %fusion.62) | copy-start | bytes 7077892
  89.9 4.5 %copy-start.5 = (f32[6,3,32,128]{3,2,1,0:T(8,128)}, f32[6,3,32,128]{3,2,1,0:T(8,128)S(1)}, u32[]{:S(2)}) copy-start(f32[6,3,32,128]{3,2,1,0:T(8,128)S(1)} %get-tuple-element.24) | copy-start | bytes 884740
  91.2 2.4 %copy-start.13 = (f32[8,6,3,32,128]{4,3,2,1,0:T(8,128)}, f32[8,6,3,32,128]{4,3,2,1,0:T(8,128)S(1)}, u32[]{:S(2)}) copy-start(f32[8,6,3,32,128]{4,3,2,1,0:T(8,128)S(1)} %get-tuple-element.41) | copy-start | bytes 7077892
  91.5 2.9 %copy-start.37 = (f32[3,32,128]{2,1,0:T(8,128)S(1)}, f32[3,32,128]{2,1,0:T(8,128)}, u32[]{:S(2)}) copy-start(f32[3,32,128]{2,1,0:T(8,128)} %copy-done.36) | copy-start | bytes 147460
  91.5 2.9 %copy-start.40 = (f32[3,32,128]{2,1,0:T(8,128)S(1)}, f32[3,32,128]{2,1,0:T(8,128)}, u32[]{:S(2)}) copy-start(f32[3,32,128]{2,1,0:T(8,128)} %copy-done.39) | copy-start | bytes 147460
  91.5 2.9 %copy-start.43 = (f32[3,32,128]{2,1,0:T(8,128)S(1)}, f32[3,32,128]{2,1,0:T(8,128)}, u32[]{:S(2)}) copy-start(f32[3,32,128]{2,1,0:T(8,128)} %copy-done.42) | copy-start | bytes 147460
  93.7 2.0 %copy-start.10 = (f32[2,3,32,128]{3,2,1,0:T(8,128)S(1)}, f32[2,3,32,128]{3,2,1,0:T(8,128)}, u32[]{:S(2)}) copy-start(f32[2,3,32,128]{3,2,1,0:T(8,128)} %copy.241) | copy-start | bytes 294916
  94.3 2.4 %copy-start.28 = (f32[6,3,32,128]{3,2,1,0:T(8,128)}, f32[6,3,32,128]{3,2,1,0:T(8,128)S(1)}, u32[]{:S(2)}) copy-start(f32[6,3,32,128]{3,2,1,0:T(8,128)S(1)} %get-tuple-element.99) | copy-start | bytes 884740
  94.3 2.4 %copy-start.34 = (f32[6,3,32,128]{3,2,1,0:T(8,128)}, f32[6,3,32,128]{3,2,1,0:T(8,128)S(1)}, u32[]{:S(2)}) copy-start(f32[6,3,32,128]{3,2,1,0:T(8,128)S(1)} %get-tuple-element.100) | copy-start | bytes 884740
  94.4 19.5 %slice-start.2 = ((s8[5505024]{0:T(1024)(128)(4,1)}), s8[1310720]{0:T(1024)(128)(4,1)S(1)}, s32[]{:S(2)}) async-start(s8[5505024]{0:T(1024)(128)(4,1)} %bitcast.48), calls=%async_computation.2 | async-start | bytes 2621440
  98.0 9.4 %collective-permute-start.3 = (f32[9,2,5,1,128]{4,1,3,2,0:T(2,128)}, f32[9,2,5,1,128]{4,1,3,2,0:T(2,128)}, u32[]{:S(2)}, u32[]{:S(2)}) collective-permute-start(f32[9,2,5,1,128]{4,1,3,2,0:T(2,128)} %copy.243), channel_id=1, source_target_pairs={{1,0},{2,1},{3,2},{5,4},{6,5},{7,6},{9,8},{10,9},{11,10},{13,12},{... | collective-permute-start | bytes 138248 | tf_op jit(solution)/shard_map/ppermute | solution.py:22
  101.3 7.1 %collective-permute-start.2 = (f32[9,2,5,1,128]{4,1,3,2,0:T(2,128)}, f32[9,2,5,1,128]{4,1,3,2,0:T(2,128)}, u32[]{:S(2)}, u32[]{:S(2)}) collective-permute-start(f32[9,2,5,1,128]{4,1,3,2,0:T(2,128)} %copy.242), channel_id=1, source_target_pairs={{0,1},{1,2},{2,3},{4,5},{5,6},{6,7},{8,9},{9,10},{10,11},{12,13},{... | collective-permute-start | bytes 138248 | tf_op jit(solution)/shard_map/ppermute | solution.py:21
  105.8 7.6 %copy-start.17 = (f32[3,32,128]{2,1,0:T(8,128)S(1)}, f32[3,32,128]{2,1,0:T(8,128)}, u32[]{:S(2)}) copy-start(f32[3,32,128]{2,1,0:T(8,128)} %copy-done.16) | copy-start | bytes 147460
  107.4 5.9 %copy-start = (f32[8,8,3,32,128]{4,3,2,1,0:T(8,128)S(1)}, f32[8,8,3,32,128]{4,3,2,1,0:T(8,128)}, u32[]{:S(2)}) copy-start(f32[8,8,3,32,128]{4,3,2,1,0:T(8,128)} %broadcast_multiply_fusion) | copy-start | bytes 9437188
  109.3 4.6 %slice-start.3 = ((s8[5505024]{0:T(1024)(128)(4,1)}), s8[4194304]{0:T(1024)(128)(4,1)S(1)}, s32[]{:S(2)}) async-start(s8[5505024]{0:T(1024)(128)(4,1)} %bitcast.48), calls=%async_computation.3 | async-start | bytes 8388608
  112.3 43.3 %copy-start.3 = (f32[2,3,32,128]{3,2,1,0:T(8,128)}, f32[2,3,32,128]{3,2,1,0:T(8,128)S(1)}, u32[]{:S(2)}) copy-start(f32[2,3,32,128]{3,2,1,0:T(8,128)S(1)} %get-tuple-element.21) | copy-start | bytes 294916
  112.3 43.3 %copy-start.26 = (f32[2,3,32,128]{3,2,1,0:T(8,128)}, f32[2,3,32,128]{3,2,1,0:T(8,128)S(1)}, u32[]{:S(2)}) copy-start(f32[2,3,32,128]{3,2,1,0:T(8,128)S(1)} %get-tuple-element.22) | copy-start | bytes 294916
  117.6 4.4 %copy-start.1 = (f32[8,6,3,32,128]{4,3,2,1,0:T(8,128)}, f32[8,6,3,32,128]{4,3,2,1,0:T(8,128)S(1)}, u32[]{:S(2)}) copy-start(f32[8,6,3,32,128]{4,3,2,1,0:T(8,128)S(1)} %fusion.10) | copy-start | bytes 7077892
  117.7 2.5 %copy-start.14 = (f32[8,6,3,32,128]{4,3,2,1,0:T(8,128)S(1)}, f32[8,6,3,32,128]{4,3,2,1,0:T(8,128)}, u32[]{:S(2)}) copy-start(f32[8,6,3,32,128]{4,3,2,1,0:T(8,128)} %copy-done.13) | copy-start | bytes 7077892
  117.7 2.5 %copy-start.31 = (f32[6,3,32,128]{3,2,1,0:T(8,128)S(1)}, f32[6,3,32,128]{3,2,1,0:T(8,128)}, u32[]{:S(2)}) copy-start(f32[6,3,32,128]{3,2,1,0:T(8,128)} %copy-done.30) | copy-start | bytes 884740
  117.7 2.5 %copy-start.41 = (f32[3,32,128]{2,1,0:T(8,128)S(1)}, f32[3,32,128]{2,1,0:T(8,128)}, u32[]{:S(2)}) copy-start(f32[3,32,128]{2,1,0:T(8,128)} %copy-done.39) | copy-start | bytes 147460
  117.7 2.6 %copy-start.51 = (f32[6,3,32,128]{3,2,1,0:T(8,128)S(1)}, f32[6,3,32,128]{3,2,1,0:T(8,128)}, u32[]{:S(2)}) copy-start(f32[6,3,32,128]{3,2,1,0:T(8,128)} %get-tuple-element.32) | copy-start | bytes 884740
  123.8 9.0 %slice-start.4 = ((f32[8,6,3,32,128]{4,3,2,1,0:T(8,128)}), f32[8,5,3,32,128]{4,3,2,1,0:T(8,128)S(1)}, s32[]{:S(2)}) async-start(f32[8,6,3,32,128]{4,3,2,1,0:T(8,128)} %copy-done.1), calls=%async_computation.4 | async-start | bytes 3932160 | tf_op jit(solution)/shard_map/slice | solution.py:28
  123.8 9.0 %slice-start.5 = ((f32[8,6,3,32,128]{4,3,2,1,0:T(8,128)}), f32[8,5,3,32,128]{4,3,2,1,0:T(8,128)S(1)}, s32[]{:S(2)}) async-start(f32[8,6,3,32,128]{4,3,2,1,0:T(8,128)} %copy-done.2), calls=%async_computation.5 | async-start | bytes 3932160 | tf_op jit(solution)/shard_map/slice | solution.py:28
  125.9 18.9 %collective-permute-start.4 = (f32[9,2,1,32,128]{4,3,2,1,0:T(8,128)S(1)}, f32[9,2,1,32,128]{4,3,2,1,0:T(8,128)S(1)}, u32[]{:S(2)}, u32[]{:S(2)}) collective-permute-start(f32[9,2,1,32,128]{4,3,2,1,0:T(8,128)S(1)} %get-tuple-element.87), channel_id=1, source_target_pairs={{0,4},{4,8},{8,12},{12,16},{16,20},{20,24},{24,28},{1,5},{5,9},{9,... | collective-permute-start | bytes 884744 | tf_op jit(solution)/shard_map/ppermute | solution.py:21
  128.2 16.6 %collective-permute-start.5 = (f32[9,2,1,32,128]{4,3,2,1,0:T(8,128)S(1)}, f32[9,2,1,32,128]{4,3,2,1,0:T(8,128)S(1)}, u32[]{:S(2)}, u32[]{:S(2)}) collective-permute-start(f32[9,2,1,32,128]{4,3,2,1,0:T(8,128)S(1)} %get-tuple-element.88), channel_id=1, source_target_pairs={{4,0},{8,4},{12,8},{16,12},{20,16},{24,20},{28,24},{5,1},{9,5},{13... | collective-permute-start | bytes 884744 | tf_op jit(solution)/shard_map/ppermute | solution.py:22
  135.3 1.5 copy-start.54
  142.0 8.8 %copy-start.55 = (f32[5,3,32,128]{3,2,1,0:T(8,128)S(1)}, f32[5,3,32,128]{3,2,1,0:T(8,128)}, u32[]{:S(2)}) copy-start(f32[5,3,32,128]{3,2,1,0:T(8,128)} %slice.881) | copy-start | bytes 737284
  142.0 8.8 %copy-start.56 = (f32[5,3,32,128]{3,2,1,0:T(8,128)S(1)}, f32[5,3,32,128]{3,2,1,0:T(8,128)}, u32[]{:S(2)}) copy-start(f32[5,3,32,128]{3,2,1,0:T(8,128)} %slice.889) | copy-start | bytes 737284
  144.9 10.7 %copy-start.62 = (f32[1,3,32,128]{3,2,1,0:T(8,128)S(1)}, f32[1,3,32,128]{3,2,1,0:T(8,128)}, u32[]{:S(2)}) copy-start(f32[1,3,32,128]{3,2,1,0:T(8,128)} %get-tuple-element.101) | copy-start | bytes 147460
  144.9 10.7 %copy-start.63 = (f32[1,3,32,128]{3,2,1,0:T(8,128)S(1)}, f32[1,3,32,128]{3,2,1,0:T(8,128)}, u32[]{:S(2)}) copy-start(f32[1,3,32,128]{3,2,1,0:T(8,128)} %get-tuple-element.102) | copy-start | bytes 147460
  145.0 6.3 %collective-permute-start.7 = (f32[9,2,5,1,128]{4,1,3,2,0:T(2,128)S(1)}, f32[9,2,5,1,128]{4,1,3,2,0:T(2,128)S(1)}, u32[]{:S(2)}, u32[]{:S(2)}) collective-permute-start(f32[9,2,5,1,128]{4,1,3,2,0:T(2,128)S(1)} %copy.247), channel_id=1, source_target_pairs={{1,0},{2,1},{3,2},{5,4},{6,5},{7,6},{9,8},{10,9},{11,10},{13,12},{... | collective-permute-start | bytes 138248 | tf_op jit(solution)/shard_map/ppermute | solution.py:22
  149.5 6.0 %collective-permute-start.6 = (f32[9,2,5,1,128]{4,1,3,2,0:T(2,128)S(1)}, f32[9,2,5,1,128]{4,1,3,2,0:T(2,128)S(1)}, u32[]{:S(2)}, u32[]{:S(2)}) collective-permute-start(f32[9,2,5,1,128]{4,1,3,2,0:T(2,128)S(1)} %copy.246), channel_id=1, source_target_pairs={{0,1},{1,2},{2,3},{4,5},{5,6},{6,7},{8,9},{9,10},{10,11},{12,13},{... | collective-permute-start | bytes 138248 | tf_op jit(solution)/shard_map/ppermute | solution.py:21
  (25 other events, 28.6 us)
where the time goes:
time: 166 us; the launch traced here: 165 us
  other arithmetic  52.5 us (32%)
  local copies, waits for them, and re-layouts  48.9 us (29%)
  blocking collectives  32.7 us (20%)
  starting transfers between devices  24 us (14%)
  waiting for transfers between devices  4.48 us (3%)
  between operations  1.88 us (1%)
    unnamed x181, local copies, waits for them, and re-layouts  36.2 us
    all_gather x1, blocking collectives, shards(): current = lax.all_gather(state, 'param', axis=3, tiled=True)  32.7 us
    ppermute x4, starting transfers between devices, padded_2(): after = lax.ppermute(first, axis, down)  16 us
    unnamed x32, other arithmetic  11.5 us
    slice x14, local copies, waits for them, and re-layouts, field_slice(): return values[..., lower_end:upper_end, :, :, :]  9.28 us
    sub x4, other arithmetic, pellet_tangent(): tangent_diffusion * shell_flux(pore_conc)  8.14 us
    ppermute x4, starting transfers between devices, padded_2(): before = lax.ppermute(last, axis, up)  8.03 us
    concatenate x1, other arithmetic, advance_tangent(): return jnp.concatenate([new_bulk, new_pores], axis=-4)  5.56 us
  transfers between devices with their start and end apart: 8, of which 2 were waited for; matrix products, arithmetic and copies ran while one was open for 39% of the time, Pallas kernels for 0%

commit v1 on v0

v1 whole, which is shorter than its diff:
```python
import jax
import jax.numpy as jnp
from jax import lax
from jax.experimental import pallas as pl
from jax.experimental.pallas import tpu as pltpu
from jax.sharding import PartitionSpec as P

DT = 0.15
AHEAD = DT * 0.5
BEHIND = DT * 1.5
SIDE = DT * 0.25
CENTER = 1.0 - DT * 3.0
FILM = DT * 1.5
G = (0.3, 0.6, 0.9, 1.2, 1.5)
F32 = jnp.float32

NP = 8
NB = 12
NG = 12

X0 = 0
X1 = X0 + 8
HS = X1 + 16
RS = HS + 2
Y0 = RS + 2
Y0S = Y0 + 2
Y1 = Y0S + 2
GA = Y1 + 18
GB = GA + 9
MESSAGES = GB + 7


def kernel(
    st_in, sens, pack, zone, coef, targ, st_out, out,
    sv, gst, hsend, hrecv, rsend, rrecv, turn,
    s0, s1, s2, th, ev, kv, pc, av, bv, gv,
    hx0, hx1, bb, bs, c1, p51, yb0, yr0, yb1, yr1,
    ss, rs, lsem,
):
    me, sl, ti = (lax.axis_index(a) for a in ("param", "slab", "tile"))
    h, c = lax.div(me, 2), lax.rem(me, 2)
    jp = lax.rem(h + 1, 4) * 2 + c
    jm = lax.rem(h + 3, 4) * 2 + c
    jo = lax.rem(h + 2, 4) * 2 + c
    other = 1 - 2 * c
    has_dn, has_up = sl > 0, sl < 7
    has_lo, has_hi = ti > 0, ti < 3
    up, dn = (me, sl + 1, ti), (me, sl - 1, ti)
    hi, lo = (me, sl, ti + 1), (me, sl, ti - 1)
    right, left, sib = (jp, sl, ti), (jm, sl, ti), (me + other, sl, ti)

    def loop(n, body):
        lax.fori_loop(0, n, lambda i, carry: (body(i), carry)[1], 0)

    def remote(src, dst, number, device):
        return pltpu.make_async_remote_copy(
            src_ref=src, dst_ref=dst, send_sem=ss.at[number], recv_sem=rs.at[number],
            device_id=device, device_id_type=pl.DeviceIdType.MESH,
        )

    bulk_copy = pltpu.make_async_copy(sens.at[:, pl.ds(0, 2)], sv.at[:, pl.ds(0, 2)], lsem.at[NP])
    bulk_copy.start()

    def shell_copy(p):
        return pltpu.make_async_copy(
            sens.at[p, pl.ds(2, 12)], sv.at[p, pl.ds(2, 12)], lsem.at[p]
        )

    loop(NP, lambda p: shell_copy(p).start())

    mine = pl.multiple_of(me * 16, 16)
    blank = jnp.zeros((16, 32), F32)
    for g in range(11):
        parts = [st_in[4 * g + k] if 4 * g + k < 42 else blank for k in range(4)]
        gst[g, pl.ds(mine, 16), :] = jnp.concatenate(parts, axis=-1)
    hsend[...] = jnp.concatenate([st_in[q] for q in (2, 5, 0, 3)], axis=-1)

    barrier = pltpu.get_barrier_semaphore()

    def greet(device):
        pl.semaphore_signal(barrier, inc=1, device_id=device, device_id_type=pl.DeviceIdType.MESH)

    for device in (right, left, sib):
        greet(device)
    for present, device in ((has_up, up), (has_dn, dn), (has_hi, hi), (has_lo, lo)):
        pl.when(present)(lambda device=device: greet(device))
    present_count = sum(x.astype(jnp.int32) for x in (has_up, has_dn, has_hi, has_lo))
    pl.semaphore_wait(barrier, 3 + present_count)

    class Pair:
        def __init__(self, number, srcs, dsts, slab):
            plus, minus = (up, dn) if slab else (hi, lo)
            self.to_plus, self.to_minus = (has_up, has_dn) if slab else (has_hi, has_lo)
            self.a = remote(srcs[0], dsts[0], number, plus)
            self.b = remote(srcs[1], dsts[1], number + 1, minus)

        def start(self):
            pl.when(self.to_plus)(lambda: self.a.start())
            pl.when(self.to_minus)(lambda: self.b.start())

        def wait_recv(self):
            pl.when(self.to_minus)(lambda: self.a.wait_recv())
            pl.when(self.to_plus)(lambda: self.b.wait_recv())

        def wait_send(self):
            pl.when(self.to_plus)(lambda: self.a.wait_send())
            pl.when(self.to_minus)(lambda: self.b.wait_send())

    halo_state = Pair(HS, (hsend, hsend), (hrecv.at[0], hrecv.at[1]), True)

    def halo0(k):
        two, bulk = pl.ds(2 * k, 2), pl.ds(0, 2)
        return Pair(
            X0 + 2 * k,
            (sens.at[two, bulk, pl.ds(8, 4)], sens.at[two, bulk, pl.ds(0, 4)]),
            (hx0.at[0, two], hx0.at[1, two]),
            True,
        )

    def halo1(p):
        return Pair(
            X1 + 2 * p,
            (bb.at[p, :, pl.ds(8, 4)], bb.at[p, :, pl.ds(0, 4)]),
            (hx1.at[0, p], hx1.at[1, p]),
            True,
        )

    partial_state = Pair(RS, (rsend, rsend), (rrecv.at[0], rrecv.at[1]), True)
    eight = pl.ds(0, NP)
    rows0 = Pair(Y0, (yb0.at[0, eight], yb0.at[1, eight]), (yr0.at[0, eight], yr0.at[1, eight]), False)
    rows0s = Pair(Y0S, (yb0.at[0, NP], yb0.at[1, NP]), (yr0.at[0, NP], yr0.at[1, NP]), False)

    def rows1(q):
        return Pair(Y1 + 2 * q, (yb1.at[0, q], yb1.at[1, q]), (yr1.at[0, q], yr1.at[1, q]), False)

    def shard(j, first, count):
        return gst.at[pl.ds(first, count), pl.ds(pl.multiple_of(j * 16, 16), 16)]

    def pass_on(j, first, count, number, device):
        ref = shard(j, first, count)
        return remote(ref, ref, number, device)

    send_a = [
        pass_on(me, 0, 11, GA, right), pass_on(me, 0, 11, GA + 1, left), pass_on(me, 0, 11, GA + 2, sib),
        pass_on(jm, 0, 6, GA + 3, right), pass_on(jm, 0, 11, GA + 4, sib),
        pass_on(jp, 6, 5, GA + 5, left), pass_on(jp, 0, 11, GA + 6, sib),
        pass_on(jo, 0, 6, GA + 7, sib), pass_on(jo, 6, 5, GA + 8, sib),
    ]
    recv_a = [
        pass_on(jm, 0, 11, GA, right), pass_on(jp, 0, 11, GA + 1, left), pass_on(me + other, 0, 11, GA + 2, sib),
        pass_on(jo, 0, 6, GA + 3, right), pass_on(jm + other, 0, 11, GA + 4, sib),
        pass_on(jo, 6, 5, GA + 5, left), pass_on(jp + other, 0, 11, GA + 6, sib),
        pass_on(jo + other, 0, 6, GA + 7, sib), pass_on(jo + other, 6, 5, GA + 8, sib),
    ]
    send_b = [
        pass_on(me, 11, 1, GB, right), pass_on(me, 11, 1, GB + 1, left), pass_on(me, 11, 1, GB + 2, sib),
        pass_on(jm, 11, 1, GB + 3, right), pass_on(jm, 11, 1, GB + 4, sib),
        pass_on(jp, 11, 1, GB + 5, sib), pass_on(jo, 11, 1, GB + 6, sib),
    ]
    recv_b = [
        pass_on(jm, 11, 1, GB, right), pass_on(jp, 11, 1, GB + 1, left), pass_on(me + other, 11, 1, GB + 2, sib),
        pass_on(jo, 11, 1, GB + 3, right), pass_on(jm + other, 11, 1, GB + 4, sib),
        pass_on(jp + other, 11, 1, GB + 5, sib), pass_on(jo + other, 11, 1, GB + 6, sib),
    ]

    halo_state.start()
    for k in range(3):
        send_a[k].start()
    loop(4, lambda k: halo0(k).start())

    def clear(ref, k):
        ref[k] = jnp.zeros(ref.shape[1:], F32)

    for absent, k in ((jnp.logical_not(has_dn), 0), (jnp.logical_not(has_up), 1)):
        @pl.when(absent)
        def _(k=k):
            for ref in (hrecv, rrecv):
                clear(ref, k)
            def one(p):
                hx0[k, p] = jnp.zeros(hx0.shape[2:], F32)
                hx1[k, p] = jnp.zeros(hx1.shape[2:], F32)
            loop(NP, one)
    for absent, k in ((jnp.logical_not(has_lo), 0), (jnp.logical_not(has_hi), 1)):
        @pl.when(absent)
        def _(k=k):
            clear(yr0, k)
            clear(yr1, k)

    def cell_theta(b):
        z = zone[b]
        is_zone = [z == j for j in range(1, 8)]
        values = []
        for k in range(8):
            v = jnp.full((8, 128), coef[k, 0], F32)
            for j in range(1, 8):
                v = jnp.where(is_zone[j - 1], coef[k, j], v)
            th[b, k] = v
            values.append(v)
        for i in range(2):
            exchange = DT * values[i] * pack[b]
            kv[i, b] = exchange
            pc[i, b] = CENTER - exchange
            for s in range(5):
                ev[b, 5 * i + s] = (DT * G[s]) * values[2 + i]

    loop(NB, cell_theta)

    bulk_copy.wait()

    def pack_rows0(p):
        for i in range(2):
            for x in range(3):
                r = 3 * i + x
                yb0[0, p, pl.ds(r, 1), :] = sv[p, i, 4 * x + 3, pl.ds(7, 1), :]
                yb0[1, p, pl.ds(r, 1), :] = sv[p, i, 4 * x, pl.ds(0, 1), :]

    loop(NP, pack_rows0)
    rows0.start()

    lane16 = lax.broadcasted_iota(jnp.int32, (16, 128), 1)
    halo_state.wait_recv()
    gst[11, pl.ds(mine, 16), :] = jnp.where(lane16 < 64, hrecv[0], hrecv[1])
    for k in range(3):
        send_b[k].start()
    recv_a[0].wait_recv()
    send_a[3].start()
    send_a[4].start()
    recv_a[1].wait_recv()
    send_a[5].start()
    send_a[6].start()
    recv_b[0].wait_recv()
    send_b[3].start()
    send_b[4].start()
    recv_b[1].wait_recv()
    send_b[5].start()
    recv_a[3].wait_recv()
    send_a[7].start()
    recv_a[5].wait_recv()
    send_a[8].start()
    recv_b[3].wait_recv()
    send_b[6].start()
    for k in (2, 4, 6, 7, 8):
        recv_a[k].wait_recv()
    for k in (2, 4, 5, 6):
        recv_b[k].wait_recv()

    def unpack(g):
        s0[pl.ds(16 * g, 16)] = gst[g].T.reshape(16, 8, 128)

    loop(NG, unpack)

    def state_rows(state, buffer):
        for i in range(2):
            for x in range(3):
                r = 3 * i + x
                buffer[0, NP, pl.ds(r, 1), :] = state[i * NB + 4 * x + 3, pl.ds(7, 1), :]
                buffer[1, NP, pl.ds(r, 1), :] = state[i * NB + 4 * x, pl.ds(0, 1), :]

    state_rows(s0, yb0)
    rows0s.start()

    def zero_tables(b):
        for n in range(2):
            gv[n, b] = jnp.zeros(gv.shape[2:], F32)

    loop(NB, zero_tables)

    def tables(n, now, later):
        def block(b):
            kf, dp, qm, bb_ = ([th[b, 2 * k + i] for i in range(2)] for k in range(4))
            conc = [now[i * NB + b] for i in range(2)]
            pore = [[now[(2 + 6 * i + s) * NB + b] for s in range(6)] for i in range(2)]
            cap = [qm[i] * bb_[i] for i in range(2)]
            film = [FILM * kf[i] for i in range(2)]
            for s in range(6):
                inverse = 1.0 / (1.0 + bb_[0] * pore[0][s] + bb_[1] * pore[1][s])
                u = [pore[i][s] * inverse for i in range(2)]
                for i in range(2):
                    f = 2 + 6 * i + s
                    rate = DT * cap[i] * inverse
                    kept = 1.0 - bb_[i] * u[i]
                    own = 1.0 - rate * kept
                    if s == 5:
                        own = own - film[i]
                    av[n, b, 6 * i + s] = own
                    bv[n, b, 6 * i + s] = rate * u[i] * bb_[1 - i]
                    if s == 0:
                        flux = G[0] * (pore[i][1] - pore[i][0])
                    elif s == 5:
                        flux = -(G[4] * (pore[i][5] - pore[i][4]))
                    else:
                        flux = G[s] * (pore[i][s + 1] - pore[i][s]) - G[s - 1] * (pore[i][s] - pore[i][s - 1])
                    gv[n, b, 2 + i, f] = DT * flux
                    gv[n, b, 4 + i, f] = -(DT * bb_[i]) * u[i]
                    gv[n, b, 6 + i, f] = -(DT * qm[i]) * u[i] * kept
                    gv[n, b, 7 - i, f] = DT * cap[i] * u[i] * u[1 - i]
                    fresh = pore[i][s] + DT * dp[i] * flux - DT * cap[i] * u[i]
                    if s == 5:
                        gap = conc[i] - pore[i][5]
                        gv[n, b, i, f] = FILM * gap
                        gv[n, b, i, i] = -(DT * pack[b]) * gap
                        fresh = fresh + film[i] * gap
                    later[f * NB + b] = fresh

        loop(NB, block)

    tables(0, s0, s1)

    row = lax.broadcasted_iota(jnp.int32, (32, 128), 0)
    lane = lax.broadcasted_iota(jnp.int32, (32, 128), 1)

    def around(v, below, above):
        return (
            jnp.where(row == 0, below, pltpu.roll(v, 1, 0))
            + jnp.where(row == 31, above, pltpu.roll(v, 31, 0))
            + jnp.where(lane == 0, 0.0, pltpu.roll(v, 1, 1))
            + jnp.where(lane == 127, 0.0, pltpu.roll(v, 127, 1))
        )

    def plane(values):
        return values.reshape(32, 128)

    def advance(i, planes, outer, below, above):
        result = []
        for x in range(3):
            four = pl.ds(4 * x, 4)
            v = planes[x]
            w = plane(pc[i, four]) * v + plane(kv[i, four]) * plane(outer(x)) + SIDE * around(v, below(x), above(x))
            if x > 0:
                w = w + BEHIND * planes[x - 1]
            if x < 2:
                w = w + AHEAD * planes[x + 1]
            result.append(w)
        return result

    def forcing(n, p, i, x):
        t = targ[p]
        four = pl.ds(4 * x, 4)
        return jnp.where(zone[four] == lax.rem(t, 8), gv[n, four, lax.div(t, 8), i], 0.0).reshape(32, 128)

    rows0.wait_recv()

    def partial(p):
        for i in range(2):
            planes = [plane(sv[p, i, pl.ds(4 * x, 4)]) for x in range(3)]
            fresh = advance(
                i, planes, lambda x: sv[p, 7 + 6 * i, pl.ds(4 * x, 4)],
                lambda x: yr0[0, p, pl.ds(3 * i + x, 1), :], lambda x: yr0[1, p, pl.ds(3 * i + x, 1), :],
            )
            for x in range(3):
                bb[p, i, pl.ds(4 * x, 4)] = (fresh[x] + forcing(0, p, i, x)).reshape(4, 8, 128)

    def partial_and_send(p):
        shell_copy(p).wait()
        partial(p)
        halo1(p).start()

    loop(NP, partial_and_send)

    rows0s.wait_recv()
    for i in range(2):
        planes = [plane(s0[pl.ds(i * NB + 4 * x, 4)]) for x in range(3)]
        fresh = advance(
            i, planes, lambda x: s0[pl.ds((7 + 6 * i) * NB + 4 * x, 4)],
            lambda x: yr0[0, NP, pl.ds(3 * i + x, 1), :], lambda x: yr0[1, NP, pl.ds(3 * i + x, 1), :],
        )
        bs[pl.ds(4 * i, 4)] = fresh[2].reshape(4, 8, 128)
        bs[pl.ds(8 + 4 * i, 4)] = fresh[0].reshape(4, 8, 128)
        s1[pl.ds(i * NB, 4)] = fresh[0].reshape(4, 8, 128) + BEHIND * s0[pl.ds(176 + 4 * i, 4)]
        s1[pl.ds(i * NB + 4, 4)] = fresh[1].reshape(4, 8, 128)
        s1[pl.ds(i * NB + 8, 4)] = fresh[2].reshape(4, 8, 128) + AHEAD * s0[pl.ds(184 + 4 * i, 4)]
    state_rows(s1, yb1)
    rows1(NP).start()
    turn[...] = bs[...].reshape(128, 128).T
    rsend[...] = turn[pl.ds(mine, 16), :]
    partial_state.start()
    tables(1, s1, s2)

    def whole(p):
        for i in range(2):
            c1[p, i, pl.ds(0, 4)] = bb[p, i, pl.ds(0, 4)] + BEHIND * hx0[0, p, i]
            c1[p, i, pl.ds(4, 4)] = bb[p, i, pl.ds(4, 4)]
            c1[p, i, pl.ds(8, 4)] = bb[p, i, pl.ds(8, 4)] + AHEAD * hx0[1, p, i]
            for x in range(3):
                r = 3 * i + x
                yb1[0, p, pl.ds(r, 1), :] = c1[p, i, 4 * x + 3, pl.ds(7, 1), :]
                yb1[1, p, pl.ds(r, 1), :] = c1[p, i, 4 * x, pl.ds(0, 1), :]
        rows1(p).start()

    def shells(p):
        t = targ[p]
        kind, target_zone = lax.div(t, 8), lax.rem(t, 8)

        def block(b):
            within = zone[b] == target_zone
            t_now = [[sv[p, 2 + 6 * i + s, b] for s in range(6)] for i in range(2)]
            for n in range(2):
                bulk = sv if n == 0 else c1
                t_later = []
                for i in range(2):
                    flux = [ev[b, 5 * i + s] * (t_now[i][s + 1] - t_now[i][s]) for s in range(5)]
                    fresh = []
                    for s in range(6):
                        v = av[n, b, 6 * i + s] * t_now[i][s] + bv[n, b, 6 * i + s] * t_now[1 - i][s]
                        if s < 5:
                            v = v + flux[s]
                        if s > 0:
                            v = v - flux[s - 1]
                        if s == 5:
                            v = v + FILM * th[b, i] * bulk[p, i, b]
                        fresh.append(v + jnp.where(within, gv[n, b, kind, 2 + 6 * i + s], 0.0))
                    t_later.append(fresh)
                t_now = t_later
                if n == 0:
                    for i in range(2):
                        p51[p, i, b] = t_now[i][5]
            for i in range(2):
                for s in range(6):
                    out[p, 2 + 6 * i + s, b] = t_now[i][s]

        loop(NB, block)

    def step_chunk(k):
        halo0(k).wait_recv()
        for j in range(2):
            whole(2 * k + j)
        loop(2, lambda j: shells(2 * k + j))

    loop(4, step_chunk)

    from_dn = (BEHIND * AHEAD) * has_dn.astype(F32)
    from_up = (BEHIND * AHEAD) * has_up.astype(F32)

    def second(p):
        rows1(p).wait_recv()
        for i in range(2):
            planes = [plane(c1[p, i, pl.ds(4 * x, 4)]) for x in range(3)]
            fresh = advance(
                i, planes, lambda x: p51[p, i, pl.ds(4 * x, 4)],
                lambda x: yr1[0, p, pl.ds(3 * i + x, 1), :], lambda x: yr1[1, p, pl.ds(3 * i + x, 1), :],
            )
            fresh[0] = fresh[0] + from_dn * plane(sv[p, i, pl.ds(0, 4)])
            fresh[2] = fresh[2] + from_up * plane(sv[p, i, pl.ds(8, 4)])
            for x in range(3):
                out[p, i, pl.ds(4 * x, 4)] = (fresh[x] + forcing(1, p, i, x)).reshape(4, 8, 128)

    loop(NP, second)

    rows1(NP).wait_recv()
    for i in range(2):
        planes = [plane(s1[pl.ds(i * NB + 4 * x, 4)]) for x in range(3)]
        fresh = advance(
            i, planes, lambda x: s1[pl.ds((7 + 6 * i) * NB + 4 * x, 4)],
            lambda x: yr1[0, NP, pl.ds(3 * i + x, 1), :], lambda x: yr1[1, NP, pl.ds(3 * i + x, 1), :],
        )
        fresh[0] = fresh[0] + from_dn * plane(s0[pl.ds(i * NB, 4)])
        fresh[2] = fresh[2] + from_up * plane(s0[pl.ds(i * NB + 8, 4)])
        for x in range(3):
            s2[pl.ds(i * NB + 4 * x, 4)] = fresh[x].reshape(4, 8, 128)
    partial_state.wait_recv()
    merged = jnp.where(lane16 < 64, rrecv[0], rrecv[1])
    rolled = pltpu.roll(merged, 64, 1)
    for g in range(11):
        turn[...] = s2[pl.ds(16 * g, 16)].reshape(128, 128).T
        own = turn[pl.ds(mine, 16), :]
        if g == 0:
            own = own + jnp.where(lane16 < 32, BEHIND * merged, 0.0)
            own = own + jnp.where(lane16 >= 96, BEHIND * rolled, jnp.where(lane16 >= 64, AHEAD * merged, 0.0))
        if g == 1:
            own = own + jnp.where((lane16 >= 32) & (lane16 < 64), AHEAD * rolled, 0.0)
        for k in range(4):
            if 4 * g + k < 42:
                st_out[4 * g + k] = own[:, 32 * k : 32 * k + 32]

    def last(p):
        halo1(p).wait_recv()
        for i in range(2):
            out[p, i, pl.ds(0, 4)] = out[p, i, pl.ds(0, 4)] + BEHIND * hx1[0, p, i]
            out[p, i, pl.ds(8, 4)] = out[p, i, pl.ds(8, 4)] + AHEAD * hx1[1, p, i]

    loop(NP, last)

    halo_state.wait_send()
    partial_state.wait_send()
    rows0.wait_send()
    rows0s.wait_send()
    loop(4, lambda k: halo0(k).wait_send())
    loop(NP, lambda p: halo1(p).wait_send())
    loop(NP + 1, lambda q: rows1(q).wait_send())
    for message in send_a + send_b:
        message.wait_send()


def shards(state, sensitivity, packing, cell_zone, coefficients, param_target):
    packed = jnp.transpose(state, (0, 1, 3, 2)).reshape(42, 16, 32)
    vmem = pl.BlockSpec(memory_space=pltpu.VMEM)
    smem = pl.BlockSpec(memory_space=pltpu.SMEM)
    anywhere = pl.BlockSpec(memory_space=pl.ANY)
    scratch = [
        (NP, 14, NB, 8, 128),
        (NG, 128, 128),
        (16, 128), (2, 16, 128), (16, 128), (2, 16, 128), (128, 128),
        (192, 8, 128), (168, 8, 128), (176, 8, 128),
        (NB, 8, 8, 128), (NB, 10, 8, 128), (2, NB, 8, 128), (2, NB, 8, 128),
        (2, NB, 12, 8, 128), (2, NB, 12, 8, 128), (2, NB, 8, 14, 8, 128),
        (2, NP, 2, 4, 8, 128), (2, NP, 2, 4, 8, 128),
        (NP, 2, NB, 8, 128), (16, 8, 128), (NP, 2, NB, 8, 128), (NP, 2, NB, 8, 128),
        (2, NP + 1, 8, 128), (2, NP + 1, 8, 128), (2, NP + 1, 8, 128), (2, NP + 1, 8, 128),
    ]
    new_state, new_sens = pl.pallas_call(
        kernel,
        out_shape=(
            jax.ShapeDtypeStruct((42, 16, 32), F32),
            jax.ShapeDtypeStruct((NP, 14, NB, 8, 128), F32),
        ),
        in_specs=[vmem, anywhere, vmem, vmem, smem, smem],
        out_specs=(vmem, vmem),
        scratch_shapes=[pltpu.VMEM(shape, F32) for shape in scratch]
        + [
            pltpu.SemaphoreType.DMA((MESSAGES,)),
            pltpu.SemaphoreType.DMA((MESSAGES,)),
            pltpu.SemaphoreType.DMA((NP + 1,)),
        ],
        compiler_params=pltpu.CompilerParams(
            collective_id=0, has_side_effects=True, vmem_limit_bytes=46 * 1024 * 1024
        ),
        name="column",
    )(
        packed,
        sensitivity.reshape(NP, 14, NB, 8, 128),
        packing.reshape(NB, 8, 128),
        cell_zone.reshape(NB, 8, 128),
        coefficients,
        param_target,
    )
    new_state = jnp.transpose(new_state.reshape(14, 3, 16, 32), (0, 1, 3, 2))
    return new_state, new_sens.reshape(NP, 14, 3, 32, 128)


def solution(mesh):
    placed = (
        P(None, "slab", "tile", "param"),
        P("param", None, "slab", "tile", None),
        P("slab", "tile", None),
        P("slab", "tile", None),
        P(),
        P("param"),
    )
    return jax.shard_map(
        shards,
        mesh=mesh,
        in_specs=placed,
        out_specs=(P(None, "slab", "tile", "param"), P("param", None, "slab", "tile", None)),
        check_vma=False,
    )
```

time: 166 us -> 56.5 us (0.34)
  the two profiles are of different devices: /device:TPU:26 before, /device:TPU:35 now
where the time goes in v1:
time: 56.5 us; the launch traced here: 56.3 us
  Pallas kernels  48.5 us (86%)
  local copies, waits for them, and re-layouts  7.08 us (13%)
  between operations  0.65 us (1%)
    pallas_call x1, Pallas kernels, shards(): pl.pallas_call(kernel, out_shape=(jax.ShapeDtypeStruct((42, 16, 32), F32)...  48.5 us
    unnamed x12, local copies, waits for them, and re-layouts  7.08 us

profile of v1, /device:TPU:35, one launch (start us, length us, event | category | flops | bytes accessed | tf_op | source)
XLA Modules:
  0.0 56.3 jit_solution(11660544143527953200)
XLA Ops:
  0.6 0.0 copy-start
  0.6 1.0 %copy-done = f32[14,3,32,16]{2,3,1,0:T(8,128)S(1)} copy-done((f32[14,3,32,16]{2,3,1,0:T(8,128)S(1)}, f32[14,3,32,16]{2,3,1,0:T(8,128)}, u32[]{:S(2)}) %copy-start) | copy-done | bytes 86040
  1.6 0.0 copy-start.1
  1.6 0.8 %copy-done.1 = f32[3,32,128]{2,1,0:T(8,128)S(1)} copy-done((f32[3,32,128]{2,1,0:T(8,128)S(1)}, f32[3,32,128]{2,1,0:T(8,128)}, u32[]{:S(2)}) %copy-start.1) | copy-done | bytes 49176
  2.4 0.0 copy-start.2
  2.4 0.8 %copy-done.2 = s32[3,32,128]{2,1,0:T(8,128)S(1)} copy-done((s32[3,32,128]{2,1,0:T(8,128)S(1)}, s32[3,32,128]{2,1,0:T(8,128)}, u32[]{:S(2)}) %copy-start.2) | copy-done | bytes 49176
  3.2 0.0 copy-start.3
  3.2 0.7 %copy-done.3 = f32[8,8]{1,0:T(8,128)S(1)} copy-done((f32[8,8]{1,0:T(8,128)S(1)}, f32[8,8]{1,0:T(8,128)}, u32[]{:S(2)}) %copy-start.3) | copy-done | bytes 280
  3.9 0.0 copy-start.4
  3.9 0.7 %copy-done.4 = s32[8]{0:T(128)S(1)} copy-done((s32[8]{0:T(128)S(1)}, s32[8]{0:T(128)}, u32[]{:S(2)}) %copy-start.4) | copy-done | bytes 56
  4.6 48.5 %column.1 = (f32[42,16,32]{2,1,0:T(8,128)S(1)}, f32[8,14,12,8,128]{4,3,2,1,0:T(8,128)S(1)}) custom-call(f32[42,16,32]{2,1,0:T(8,128)S(1)} %bitcast.12, f32[8,14,12,8,128]{4,3,2,1,0:T(8,128)} %bitcast.15, f32[12,8,128]{2,1,0:T(8,128)S(1)} %bitcast.13, s32[12,8,128]{2,1,0:T(8,128)S(1)} %bitcast.14, f32[8,8]{1,0:T(8,128)S(1)} %copy-done.3, s32[8]{0:T(128)S(1)} %copy-done.4), custom_call_target="tpu_custom_call" | custom-call | tf_op jit(solution)/shard_map/column/pallas_call | solution.py:510
  53.1 0.7 %copy.10 = f32[14,3,32,16]{2,3,1,0:T(8,128)} copy(f32[14,3,32,16]{2,3,1,0:T(8,128)S(1)} %bitcast.11) | data formatting | bytes 172032
  53.8 2.4 %copy.11 = f32[8,14,3,32,128]{4,3,2,1,0:T(8,128)} copy(f32[8,14,3,32,128]{4,3,2,1,0:T(8,128)S(1)} %bitcast.10) | data formatting | bytes 11010048
Async XLA Ops:
  0.6 1.0 %copy-start = (f32[14,3,32,16]{2,3,1,0:T(8,128)S(1)}, f32[14,3,32,16]{2,3,1,0:T(8,128)}, u32[]{:S(2)}) copy-start(f32[14,3,32,16]{2,3,1,0:T(8,128)} %param.6) | copy-start | bytes 258052
  1.6 0.8 %copy-start.1 = (f32[3,32,128]{2,1,0:T(8,128)S(1)}, f32[3,32,128]{2,1,0:T(8,128)}, u32[]{:S(2)}) copy-start(f32[3,32,128]{2,1,0:T(8,128)} %param.8) | copy-start | bytes 147460
  2.4 0.8 %copy-start.2 = (s32[3,32,128]{2,1,0:T(8,128)S(1)}, s32[3,32,128]{2,1,0:T(8,128)}, u32[]{:S(2)}) copy-start(s32[3,32,128]{2,1,0:T(8,128)} %param.9) | copy-start | bytes 147460
  3.2 0.7 %copy-start.3 = (f32[8,8]{1,0:T(8,128)S(1)}, f32[8,8]{1,0:T(8,128)}, u32[]{:S(2)}) copy-start(f32[8,8]{1,0:T(8,128)} %coef.1) | copy-start | bytes 772
  3.9 0.7 %copy-start.4 = (s32[8]{0:T(128)S(1)}, s32[8]{0:T(128)}, u32[]{:S(2)}) copy-start(s32[8]{0:T(128)} %targ.1) | copy-start | bytes 100

commit v2 on v1

--- a/solution.py
+++ b/solution.py
@@ -16,25 +16,29 @@
 
 NP = 8
 NB = 12
-NG = 12
+NG = 13
 
 X0 = 0
 X1 = X0 + 8
 HS = X1 + 16
 RS = HS + 2
 Y0 = RS + 2
-Y0S = Y0 + 2
-Y1 = Y0S + 2
+YS = Y0 + 2
+Y1 = YS + 2
 GA = Y1 + 18
 GB = GA + 9
-MESSAGES = GB + 7
+GW = GB + 7
+MESSAGES = GW + 7
+SMALL = NP + 1
+LOCAL = SMALL + 5
 
 
 def kernel(
-    st_in, sens, pack, zone, coef, targ, st_out, out,
-    sv, gst, hsend, hrecv, rsend, rrecv, turn,
-    s0, s1, s2, th, ev, kv, pc, av, bv, gv,
+    st_arg, sens, pack_arg, zone_arg, coef_arg, targ_arg, st_out, out,
+    sv, gst, wst, hsend, hrecv, tile_recv, rsend, rrecv, turn,
+    s0, s1, s2, th, ev, kv, pc, av, bv, gv, gp, fw,
     hx0, hx1, bb, bs, c1, p51, yb0, yr0, yb1, yr1,
+    st_in, pack, zone, coef, targ,
     ss, rs, lsem,
 ):
     me, sl, ti = (lax.axis_index(a) for a in ("param", "slab", "tile"))
@@ -47,7 +51,7 @@
     has_lo, has_hi = ti > 0, ti < 3
     up, dn = (me, sl + 1, ti), (me, sl - 1, ti)
     hi, lo = (me, sl, ti + 1), (me, sl, ti - 1)
-    right, left, sib = (jp, sl, ti), (jm, sl, ti), (me + other, sl, ti)
+    right, left, across, sib = (jp, sl, ti), (jm, sl, ti), (jo, sl, ti), (me + other, sl, ti)
 
     def loop(n, body):
         lax.fori_loop(0, n, lambda i, carry: (body(i), carry)[1], 0)
@@ -58,15 +62,35 @@
             device_id=device, device_id_type=pl.DeviceIdType.MESH,
         )
 
+    barrier = pltpu.get_barrier_semaphore()
+
+    def greet(device):
+        pl.semaphore_signal(barrier, inc=1, device_id=device, device_id_type=pl.DeviceIdType.MESH)
+
+    for device in (right, left, across, sib):
+        greet(device)
+    for present, device in ((has_up, up), (has_dn, dn), (has_hi, hi), (has_lo, lo)):
+        pl.when(present)(lambda device=device: greet(device))
+    present_count = sum(x.astype(jnp.int32) for x in (has_up, has_dn, has_hi, has_lo))
+
     bulk_copy = pltpu.make_async_copy(sens.at[:, pl.ds(0, 2)], sv.at[:, pl.ds(0, 2)], lsem.at[NP])
-    bulk_copy.start()
 
     def shell_copy(p):
         return pltpu.make_async_copy(
             sens.at[p, pl.ds(2, 12)], sv.at[p, pl.ds(2, 12)], lsem.at[p]
         )
 
+    small = [
+        pltpu.make_async_copy(src, dst, lsem.at[SMALL + k])
+        for k, (src, dst) in enumerate(
+            ((st_arg, st_in), (pack_arg, pack), (zone_arg, zone), (coef_arg, coef), (targ_arg, targ))
+        )
+    ]
+    for copy in small:
+        copy.start()
+    bulk_copy.start()
     loop(NP, lambda p: shell_copy(p).start())
+    small[0].wait()
 
     mine = pl.multiple_of(me * 16, 16)
     blank = jnp.zeros((16, 32), F32)
@@ -74,18 +98,24 @@
         parts = [st_in[4 * g + k] if 4 * g + k < 42 else blank for k in range(4)]
         gst[g, pl.ds(mine, 16), :] = jnp.concatenate(parts, axis=-1)
     hsend[...] = jnp.concatenate([st_in[q] for q in (2, 5, 0, 3)], axis=-1)
-
-    barrier = pltpu.get_barrier_semaphore()
-
-    def greet(device):
-        pl.semaphore_signal(barrier, inc=1, device_id=device, device_id_type=pl.DeviceIdType.MESH)
-
-    for device in (right, left, sib):
-        greet(device)
-    for present, device in ((has_up, up), (has_dn, dn), (has_hi, hi), (has_lo, lo)):
-        pl.when(present)(lambda device=device: greet(device))
-    present_count = sum(x.astype(jnp.int32) for x in (has_up, has_dn, has_hi, has_lo))
-    pl.semaphore_wait(barrier, 3 + present_count)
+    wst[pl.ds(mine, 16), :] = jnp.concatenate(
+        [st_in[q] - st_in[r] for q, r in ((0, 21), (3, 39), (2, 23), (5, 41))], axis=-1
+    )
+    for copy in small[1:]:
+        copy.wait()
+
+    def zero_tables(b):
+        nothing = jnp.zeros((8, 128), F32)
+        for n in range(2):
+            for k in range(6):
+                for f in range(12):
+                    if k < 2 and f == 6 * k + 5 or k >= 2 and f // 6 == k % 2:
+                        continue
+                    gv[n, b, k, f] = nothing
+
+    loop(NB, zero_tables)
+
+    pl.semaphore_wait(barrier, 4 + present_count)
 
     class Pair:
         def __init__(self, number, srcs, dsts, slab):
@@ -128,7 +158,6 @@
     partial_state = Pair(RS, (rsend, rsend), (rrecv.at[0], rrecv.at[1]), True)
     eight = pl.ds(0, NP)
     rows0 = Pair(Y0, (yb0.at[0, eight], yb0.at[1, eight]), (yr0.at[0, eight], yr0.at[1, eight]), False)
-    rows0s = Pair(Y0S, (yb0.at[0, NP], yb0.at[1, NP]), (yr0.at[0, NP], yr0.at[1, NP]), False)
 
     def rows1(q):
         return Pair(Y1 + 2 * q, (yb1.at[0, q], yb1.at[1, q]), (yr1.at[0, q], yr1.at[1, q]), False)
@@ -152,18 +181,28 @@
         pass_on(jo, 6, 5, GA + 5, left), pass_on(jp + other, 0, 11, GA + 6, sib),
         pass_on(jo + other, 0, 6, GA + 7, sib), pass_on(jo + other, 6, 5, GA + 8, sib),
     ]
-    send_b = [
-        pass_on(me, 11, 1, GB, right), pass_on(me, 11, 1, GB + 1, left), pass_on(me, 11, 1, GB + 2, sib),
-        pass_on(jm, 11, 1, GB + 3, right), pass_on(jm, 11, 1, GB + 4, sib),
-        pass_on(jp, 11, 1, GB + 5, sib), pass_on(jo, 11, 1, GB + 6, sib),
-    ]
-    recv_b = [
-        pass_on(jm, 11, 1, GB, right), pass_on(jp, 11, 1, GB + 1, left), pass_on(me + other, 11, 1, GB + 2, sib),
-        pass_on(jo, 11, 1, GB + 3, right), pass_on(jm + other, 11, 1, GB + 4, sib),
-        pass_on(jp + other, 11, 1, GB + 5, sib), pass_on(jo + other, 11, 1, GB + 6, sib),
-    ]
-
+    tile_state = Pair(YS, (shard(me, 0, 2), shard(me, 0, 2)), (tile_recv.at[0], tile_recv.at[1]), False)
+
+    def small_gather(ref_of, number):
+        def messages(shards):
+            devices = (right, left, across, sib, sib, sib, sib)
+            return [
+                remote(ref_of(j), ref_of(j), number + k, device)
+                for k, (j, device) in enumerate(zip(shards, devices))
+            ]
+
+        return (
+            messages((me, me, me, me, jm, jp, jo)),
+            messages((jm, jp, jo, me + other, jm + other, jp + other, jo + other)),
+        )
+
+    send_b, recv_b = small_gather(lambda j: shard(j, 11, 2), GB)
+    send_w, recv_w = small_gather(lambda j: wst.at[pl.ds(pl.multiple_of(j * 16, 16), 16)], GW)
+
+    for k in range(4):
+        send_w[k].start()
     halo_state.start()
+    tile_state.start()
     for k in range(3):
         send_a[k].start()
     loop(4, lambda k: halo0(k).start())
@@ -183,8 +222,8 @@
     for absent, k in ((jnp.logical_not(has_lo), 0), (jnp.logical_not(has_hi), 1)):
         @pl.when(absent)
         def _(k=k):
-            clear(yr0, k)
-            clear(yr1, k)
+            for ref in (yr0, yr1, tile_recv):
+                clear(ref, k)
 
     def cell_theta(b):
         z = zone[b]
@@ -220,28 +259,96 @@
     lane16 = lax.broadcasted_iota(jnp.int32, (16, 128), 1)
     halo_state.wait_recv()
     gst[11, pl.ds(mine, 16), :] = jnp.where(lane16 < 64, hrecv[0], hrecv[1])
+    tile_state.wait_recv()
+    spot = lax.rem(lane16, 32)
+    gst[12, pl.ds(mine, 16), :] = jnp.where(
+        spot == 31,
+        tile_recv[0, 0],
+        jnp.where(
+            spot == 0,
+            tile_recv[1, 0],
+            jnp.where(spot == 30, pltpu.roll(tile_recv[0, 1], 127, 1), pltpu.roll(tile_recv[1, 1], 1, 1)),
+        ),
+    )
+    for k in range(4):
+        send_b[k].start()
     for k in range(3):
-        send_b[k].start()
+        recv_w[k].wait_recv()
+        send_w[4 + k].start()
     recv_a[0].wait_recv()
     send_a[3].start()
     send_a[4].start()
     recv_a[1].wait_recv()
     send_a[5].start()
     send_a[6].start()
-    recv_b[0].wait_recv()
-    send_b[3].start()
-    send_b[4].start()
-    recv_b[1].wait_recv()
-    send_b[5].start()
+
+    row = lax.broadcasted_iota(jnp.int32, (32, 128), 0)
+    lane = lax.broadcasted_iota(jnp.int32, (32, 128), 1)
+
+    def around(v, below, above):
+        return (
+            jnp.where(row == 0, below, pltpu.roll(v, 1, 0))
+            + jnp.where(row == 31, above, pltpu.roll(v, 31, 0))
+            + jnp.where(lane == 0, 0.0, pltpu.roll(v, 1, 1))
+            + jnp.where(lane == 127, 0.0, pltpu.roll(v, 127, 1))
+        )
+
+    def plane(values):
+        return values.reshape(32, 128)
+
+    def advance(i, planes, outer, below, above):
+        result = []
+        for x in range(3):
+            four = pl.ds(4 * x, 4)
+            v = planes[x]
+            w = plane(pc[i, four]) * v + plane(kv[i, four]) * plane(outer(x)) + SIDE * around(v, below(x), above(x))
+            if x > 0:
+                w = w + BEHIND * planes[x - 1]
+            if x < 2:
+                w = w + AHEAD * planes[x + 1]
+            result.append(w)
+        return result
+
+    def forcing(p, i, x, values):
+        t = targ[p]
+        target = jnp.where(lax.div(t, 8) == i, lax.rem(t, 8), -1)
+        return jnp.where(zone[pl.ds(4 * x, 4)] == target, values, 0.0)
+
+    for k in range(3, 7):
+        recv_w[k].wait_recv()
+    turned = wst[...].T.reshape(2, 2, 4, 8, 128)
+    for k in range(2):
+        for i in range(2):
+            fw[k, i] = -(DT * pack[pl.ds(8 * k, 4)]) * turned[k, i]
+    rows0.wait_recv()
+
+    def partial_and_send(p):
+        shell_copy(p).wait()
+        for i in range(2):
+            planes = [plane(sv[p, i, pl.ds(4 * x, 4)]) for x in range(3)]
+            fresh = advance(
+                i, planes, lambda x: sv[p, 7 + 6 * i, pl.ds(4 * x, 4)],
+                lambda x: yr0[0, p, pl.ds(3 * i + x, 1), :], lambda x: yr0[1, p, pl.ds(3 * i + x, 1), :],
+            )
+            for x in range(3):
+                v = fresh[x].reshape(4, 8, 128)
+                if x != 1:
+                    v = v + forcing(p, i, x, fw[x // 2, i])
+                bb[p, i, pl.ds(4 * x, 4)] = v
+        halo1(p).start()
+
+    loop(NP, partial_and_send)
+
+    for k in range(3):
+        recv_b[k].wait_recv()
+        send_b[4 + k].start()
     recv_a[3].wait_recv()
     send_a[7].start()
     recv_a[5].wait_recv()
     send_a[8].start()
-    recv_b[3].wait_recv()
-    send_b[6].start()
     for k in (2, 4, 6, 7, 8):
         recv_a[k].wait_recv()
-    for k in (2, 4, 5, 6):
+    for k in range(3, 7):
         recv_b[k].wait_recv()
 
     def unpack(g):
@@ -249,21 +356,6 @@
 
     loop(NG, unpack)
 
-    def state_rows(state, buffer):
-        for i in range(2):
-            for x in range(3):
-                r = 3 * i + x
-                buffer[0, NP, pl.ds(r, 1), :] = state[i * NB + 4 * x + 3, pl.ds(7, 1), :]
-                buffer[1, NP, pl.ds(r, 1), :] = state[i * NB + 4 * x, pl.ds(0, 1), :]
-
-    state_rows(s0, yb0)
-    rows0s.start()
-
-    def zero_tables(b):
-        for n in range(2):
-            gv[n, b] = jnp.zeros(gv.shape[2:], F32)
-
-    loop(NB, zero_tables)
 
     def tables(n, now, later):
         def block(b):
@@ -276,7 +368,7 @@
                 inverse = 1.0 / (1.0 + bb_[0] * pore[0][s] + bb_[1] * pore[1][s])
                 u = [pore[i][s] * inverse for i in range(2)]
                 for i in range(2):
-                    f = 2 + 6 * i + s
+                    f = 6 * i + s
                     rate = DT * cap[i] * inverse
                     kept = 1.0 - bb_[i] * u[i]
                     own = 1.0 - rate * kept
@@ -293,83 +385,40 @@
                     gv[n, b, 2 + i, f] = DT * flux
                     gv[n, b, 4 + i, f] = -(DT * bb_[i]) * u[i]
                     gv[n, b, 6 + i, f] = -(DT * qm[i]) * u[i] * kept
-                    gv[n, b, 7 - i, f] = DT * cap[i] * u[i] * u[1 - i]
+                    gv[n, b, 7 - i, f] = rate * pore[1 - i][s] * u[i]
                     fresh = pore[i][s] + DT * dp[i] * flux - DT * cap[i] * u[i]
                     if s == 5:
                         gap = conc[i] - pore[i][5]
                         gv[n, b, i, f] = FILM * gap
-                        gv[n, b, i, i] = -(DT * pack[b]) * gap
+                        gp[n, i, b] = -(DT * pack[b]) * gap
                         fresh = fresh + film[i] * gap
-                    later[f * NB + b] = fresh
+                    later[(2 + f) * NB + b] = fresh
 
         loop(NB, block)
 
     tables(0, s0, s1)
 
-    row = lax.broadcasted_iota(jnp.int32, (32, 128), 0)
-    lane = lax.broadcasted_iota(jnp.int32, (32, 128), 1)
-
-    def around(v, below, above):
-        return (
-            jnp.where(row == 0, below, pltpu.roll(v, 1, 0))
-            + jnp.where(row == 31, above, pltpu.roll(v, 31, 0))
-            + jnp.where(lane == 0, 0.0, pltpu.roll(v, 1, 1))
-            + jnp.where(lane == 127, 0.0, pltpu.roll(v, 127, 1))
-        )
-
-    def plane(values):
-        return values.reshape(32, 128)
-
-    def advance(i, planes, outer, below, above):
-        result = []
-        for x in range(3):
-            four = pl.ds(4 * x, 4)
-            v = planes[x]
-            w = plane(pc[i, four]) * v + plane(kv[i, four]) * plane(outer(x)) + SIDE * around(v, below(x), above(x))
-            if x > 0:
-                w = w + BEHIND * planes[x - 1]
-            if x < 2:
-                w = w + AHEAD * planes[x + 1]
-            result.append(w)
-        return result
-
-    def forcing(n, p, i, x):
-        t = targ[p]
-        four = pl.ds(4 * x, 4)
-        return jnp.where(zone[four] == lax.rem(t, 8), gv[n, four, lax.div(t, 8), i], 0.0).reshape(32, 128)
-
-    rows0.wait_recv()
-
-    def partial(p):
-        for i in range(2):
-            planes = [plane(sv[p, i, pl.ds(4 * x, 4)]) for x in range(3)]
-            fresh = advance(
-                i, planes, lambda x: sv[p, 7 + 6 * i, pl.ds(4 * x, 4)],
-                lambda x: yr0[0, p, pl.ds(3 * i + x, 1), :], lambda x: yr0[1, p, pl.ds(3 * i + x, 1), :],
-            )
-            for x in range(3):
-                bb[p, i, pl.ds(4 * x, 4)] = (fresh[x] + forcing(0, p, i, x)).reshape(4, 8, 128)
-
-    def partial_and_send(p):
-        shell_copy(p).wait()
-        partial(p)
-        halo1(p).start()
-
-    loop(NP, partial_and_send)
-
-    rows0s.wait_recv()
+    lower = ((31, 63, 95), (127, 30, 62))
+    upper = ((0, 32, 64), (96, 1, 33))
+
+    def turned_row(r):
+        return s0[192 + r // 8, pl.ds(r % 8, 1), :]
+
     for i in range(2):
         planes = [plane(s0[pl.ds(i * NB + 4 * x, 4)]) for x in range(3)]
         fresh = advance(
             i, planes, lambda x: s0[pl.ds((7 + 6 * i) * NB + 4 * x, 4)],
-            lambda x: yr0[0, NP, pl.ds(3 * i + x, 1), :], lambda x: yr0[1, NP, pl.ds(3 * i + x, 1), :],
+            lambda x: turned_row(lower[i][x]), lambda x: turned_row(upper[i][x]),
         )
         bs[pl.ds(4 * i, 4)] = fresh[2].reshape(4, 8, 128)
         bs[pl.ds(8 + 4 * i, 4)] = fresh[0].reshape(4, 8, 128)
         s1[pl.ds(i * NB, 4)] = fresh[0].reshape(4, 8, 128) + BEHIND * s0[pl.ds(176 + 4 * i, 4)]
         s1[pl.ds(i * NB + 4, 4)] = fresh[1].reshape(4, 8, 128)
         s1[pl.ds(i * NB + 8, 4)] = fresh[2].reshape(4, 8, 128) + AHEAD * s0[pl.ds(184 + 4 * i, 4)]
-    state_rows(s1, yb1)
+        for x in range(3):
+            r = 3 * i + x
+            yb1[0, NP, pl.ds(r, 1), :] = s1[i * NB + 4 * x + 3, pl.ds(7, 1), :]
+            yb1[1, NP, pl.ds(r, 1), :] = s1[i * NB + 4 * x, pl.ds(0, 1), :]
     rows1(NP).start()
     turn[...] = bs[...].reshape(128, 128).T
     rsend[...] = turn[pl.ds(mine, 16), :]
@@ -379,7 +428,7 @@
     def whole(p):
         for i in range(2):
             c1[p, i, pl.ds(0, 4)] = bb[p, i, pl.ds(0, 4)] + BEHIND * hx0[0, p, i]
-            c1[p, i, pl.ds(4, 4)] = bb[p, i, pl.ds(4, 4)]
+            c1[p, i, pl.ds(4, 4)] = bb[p, i, pl.ds(4, 4)] + forcing(p, i, 1, gp[0, i, pl.ds(4, 4)])
             c1[p, i, pl.ds(8, 4)] = bb[p, i, pl.ds(8, 4)] + AHEAD * hx0[1, p, i]
             for x in range(3):
                 r = 3 * i + x
@@ -408,7 +457,7 @@
                             v = v - flux[s - 1]
                         if s == 5:
                             v = v + FILM * th[b, i] * bulk[p, i, b]
-                        fresh.append(v + jnp.where(within, gv[n, b, kind, 2 + 6 * i + s], 0.0))
+                        fresh.append(v + jnp.where(within, gv[n, b, kind, 6 * i + s], 0.0))
                     t_later.append(fresh)
                 t_now = t_later
                 if n == 0:
@@ -442,7 +491,7 @@
             fresh[0] = fresh[0] + from_dn * plane(sv[p, i, pl.ds(0, 4)])
             fresh[2] = fresh[2] + from_up * plane(sv[p, i, pl.ds(8, 4)])
             for x in range(3):
-                out[p, i, pl.ds(4 * x, 4)] = (fresh[x] + forcing(1, p, i, x)).reshape(4, 8, 128)
+                out[p, i, pl.ds(4 * x, 4)] = fresh[x].reshape(4, 8, 128) + forcing(p, i, x, gp[1, i, pl.ds(4 * x, 4)])
 
     loop(NP, second)
 
@@ -483,29 +532,41 @@
     halo_state.wait_send()
     partial_state.wait_send()
     rows0.wait_send()
-    rows0s.wait_send()
+    tile_state.wait_send()
     loop(4, lambda k: halo0(k).wait_send())
     loop(NP, lambda p: halo1(p).wait_send())
     loop(NP + 1, lambda q: rows1(q).wait_send())
-    for message in send_a + send_b:
+    for message in send_a + send_b + send_w:
         message.wait_send()
+
+
+def write_out(st, sens, st_out, out, sems):
+    copies = [pltpu.make_async_copy(st, st_out, sems.at[NP])]
+    copies += [pltpu.make_async_copy(sens.at[p], out.at[p], sems.at[p]) for p in range(NP)]
+    for copy in copies:
+        copy.start()
+    for copy in copies:
+        copy.wait()
 
 
 def shards(state, sensitivity, packing, cell_zone, coefficients, param_target):
     packed = jnp.transpose(state, (0, 1, 3, 2)).reshape(42, 16, 32)
     vmem = pl.BlockSpec(memory_space=pltpu.VMEM)
-    smem = pl.BlockSpec(memory_space=pltpu.SMEM)
+    hbm = pl.BlockSpec(memory_space=pltpu.HBM)
     anywhere = pl.BlockSpec(memory_space=pl.ANY)
     scratch = [
         (NP, 14, NB, 8, 128),
-        (NG, 128, 128),
-        (16, 128), (2, 16, 128), (16, 128), (2, 16, 128), (128, 128),
-        (192, 8, 128), (168, 8, 128), (176, 8, 128),
+        (NG, 128, 128), (128, 128),
+        (16, 128), (2, 16, 128), (2, 2, 16, 128),
+        (16, 128), (2, 16, 128), (128, 128),
+        (208, 8, 128), (168, 8, 128), (176, 8, 128),
         (NB, 8, 8, 128), (NB, 10, 8, 128), (2, NB, 8, 128), (2, NB, 8, 128),
-        (2, NB, 12, 8, 128), (2, NB, 12, 8, 128), (2, NB, 8, 14, 8, 128),
+        (2, NB, 12, 8, 128), (2, NB, 12, 8, 128), (2, NB, 8, 12, 8, 128),
+        (2, 2, NB, 8, 128), (2, 2, 4, 8, 128),
         (2, NP, 2, 4, 8, 128), (2, NP, 2, 4, 8, 128),
         (NP, 2, NB, 8, 128), (16, 8, 128), (NP, 2, NB, 8, 128), (NP, 2, NB, 8, 128),
-        (2, NP + 1, 8, 128), (2, NP + 1, 8, 128), (2, NP + 1, 8, 128), (2, NP + 1, 8, 128),
+        (2, NP, 8, 128), (2, NP, 8, 128), (2, NP + 1, 8, 128), (2, NP + 1, 8, 128),
+        (42, 16, 32), (NB, 8, 128),
     ]
     new_state, new_sens = pl.pallas_call(
         kernel,
@@ -513,26 +574,46 @@
             jax.ShapeDtypeStruct((42, 16, 32), F32),
             jax.ShapeDtypeStruct((NP, 14, NB, 8, 128), F32),
         ),
-        in_specs=[vmem, anywhere, vmem, vmem, smem, smem],
+        in_specs=[hbm] * 6,
         out_specs=(vmem, vmem),
         scratch_shapes=[pltpu.VMEM(shape, F32) for shape in scratch]
         + [
+            pltpu.VMEM((NB, 8, 128), jnp.int32),
+            pltpu.SMEM((8, 8), F32),
+            pltpu.SMEM((NP,), jnp.int32),
             pltpu.SemaphoreType.DMA((MESSAGES,)),
             pltpu.SemaphoreType.DMA((MESSAGES,)),
-            pltpu.SemaphoreType.DMA((NP + 1,)),
+            pltpu.SemaphoreType.DMA((LOCAL,)),
         ],
         compiler_params=pltpu.CompilerParams(
             collective_id=0, has_side_effects=True, vmem_limit_bytes=46 * 1024 * 1024
         ),
         name="column",
     )(
-        packed,
-        sensitivity.reshape(NP, 14, NB, 8, 128),
-        packing.reshape(NB, 8, 128),
-        cell_zone.reshape(NB, 8, 128),
-        coefficients,
-        param_target,
+        *(
+            pltpu.with_memory_space_constraint(x, pltpu.HBM)
+            for x in (
+                packed,
+                sensitivity.reshape(NP, 14, NB, 8, 128),
+                packing.reshape(NB, 8, 128),
+                cell_zone.reshape(NB, 8, 128),
+                coefficients,
+                param_target,
+            )
+        )
     )
+    new_state, new_sens = pl.pallas_call(
+        write_out,
+        out_shape=(
+            jax.ShapeDtypeStruct((42, 16, 32), F32),
+            jax.ShapeDtypeStruct((NP, 14, NB, 8, 128), F32),
+        ),
+        in_specs=[anywhere, anywhere],
+        out_specs=(hbm, hbm),
+        scratch_shapes=[pltpu.SemaphoreType.DMA((NP + 1,))],
+        compiler_params=pltpu.CompilerParams(vmem_limit_bytes=2 * 1024 * 1024),
+        name="write_out",
+    )(new_state, new_sens)
     new_state = jnp.transpose(new_state.reshape(14, 3, 16, 32), (0, 1, 3, 2))
     return new_state, new_sens.reshape(NP, 14, 3, 32, 128)
 

time: 56.5 us -> 45.5 us (0.81)
  the two profiles are of different devices: /device:TPU:35 before, /device:TPU:1 now
where the time goes in v2:
time: 45.5 us; the launch traced here: 45.3 us
  Pallas kernels  44.7 us (98%)
  between operations  0.64 us (1%)
    pallas_call x1, Pallas kernels, shards(): pl.pallas_call(kernel, out_shape=(jax.ShapeDtypeStruct((42, 16, 32), F32)...  42.1 us
    pallas_call x1, Pallas kernels, shards(): pl.pallas_call(write_out, out_shape=(jax.ShapeDtypeStruct((42, 16, 32), F...  2.61 us

profile of v2, /device:TPU:1, one launch (start us, length us, event | category | flops | bytes accessed | tf_op | source)
XLA Modules:
  0.0 45.3 jit_solution(1596890234014381049)
XLA Ops:
  0.6 42.1 %column.1 = (f32[42,16,32]{2,1,0:T(8,128)S(1)}, f32[8,14,12,8,128]{4,3,2,1,0:T(8,128)S(1)}) custom-call(f32[42,16,32]{2,1,0:T(8,128)} %bitcast.11, f32[8,14,12,8,128]{4,3,2,1,0:T(8,128)} %bitcast.10, f32[12,8,128]{2,1,0:T(8,128)} %bitcast.12, s32[12,8,128]{2,1,0:T(8,128)} %bitcast.13, f32[8,8]{1,0:T(8,128)} %coef_arg.1, s32[8]{0:T(128)} %targ_arg.1), custom_call_target="tpu_custom_call" | custom-call | tf_op jit(solution)/shard_map/column/pallas_call | solution.py:571
  42.7 2.6 %write_out.1 = (f32[42,16,32]{2,1,0:T(8,128)}, f32[8,14,12,8,128]{4,3,2,1,0:T(8,128)}) custom-call(f32[42,16,32]{2,1,0:T(8,128)S(1)} %get-tuple-element.6.st, f32[8,14,12,8,128]{4,3,2,1,0:T(8,128)S(1)} %get-tuple-element.7.sens), custom_call_target="tpu_custom_call" | custom-call | tf_op jit(solution)/shard_map/write_out/pallas_call | solution.py:605

commit v3 on v2

--- a/solution.py
+++ b/solution.py
@@ -16,28 +16,35 @@
 
 NP = 8
 NB = 12
-NG = 13
+NG = 12
+ORDER = (0, 1, 7, 13, 2, 3, 4, 5, 6, 8, 9, 10, 11, 12)
+SETS = ((0, 6), (6, 5))
+CHUNKS = 4
 
 X0 = 0
-X1 = X0 + 8
-HS = X1 + 16
+X1 = X0 + 2 * CHUNKS
+HS = X1 + 2 * CHUNKS
 RS = HS + 2
 Y0 = RS + 2
-YS = Y0 + 2
-Y1 = YS + 2
-GA = Y1 + 18
-GB = GA + 9
-GW = GB + 7
-MESSAGES = GW + 7
+Y0S = Y0 + 2
+Y1 = Y0S + 2
+GATHER = Y1 + 18
+RELAY = GATHER + 9 * len(SETS)
+DIRECT = RELAY + 6
+MESSAGES = DIRECT + 7
 SMALL = NP + 1
 LOCAL = SMALL + 5
 
 
+def at(field):
+    return ORDER.index(field) * NB
+
+
 def kernel(
     st_arg, sens, pack_arg, zone_arg, coef_arg, targ_arg, st_out, out,
-    sv, gst, wst, hsend, hrecv, tile_recv, rsend, rrecv, turn,
-    s0, s1, s2, th, ev, kv, pc, av, bv, gv, gp, fw,
-    hx0, hx1, bb, bs, c1, p51, yb0, yr0, yb1, yr1,
+    sv, gst, hsend, hrecv, rsend, rrecv, turn,
+    s0, s1, s2, th, ev, kv, pc, av, bv, gv, gp,
+    hx0, hx1, relayed, bb, bs, c1, p51, yb0, yr0, yb1, yr1,
     st_in, pack, zone, coef, targ,
     ss, rs, lsem,
 ):
@@ -52,13 +59,20 @@
     up, dn = (me, sl + 1, ti), (me, sl - 1, ti)
     hi, lo = (me, sl, ti + 1), (me, sl, ti - 1)
     right, left, across, sib = (jp, sl, ti), (jm, sl, ti), (jo, sl, ti), (me + other, sl, ti)
+    up2, dn2 = (me, sl + 2, ti), (me, sl - 2, ti)
+    has_dn2, has_up2 = sl > 1, sl < 6
+    half, odd = lax.div(sl, 2), lax.rem(sl, 2) == 1
+    relay_up = jnp.where(odd & has_up, half + 1, 0)
+    relay_dn = jnp.where(jnp.logical_not(odd) & has_dn, 4 - half, 0)
+    relay_here = jnp.where(odd, half, jnp.maximum(3 - half, 0))
 
     def loop(n, body):
         lax.fori_loop(0, n, lambda i, carry: (body(i), carry)[1], 0)
 
-    def remote(src, dst, number, device):
+    def remote(src, dst, number, device, recv_number=None):
+        recv_number = number if recv_number is None else recv_number
         return pltpu.make_async_remote_copy(
-            src_ref=src, dst_ref=dst, send_sem=ss.at[number], recv_sem=rs.at[number],
+            src_ref=src, dst_ref=dst, send_sem=ss.at[number], recv_sem=rs.at[recv_number],
             device_id=device, device_id_type=pl.DeviceIdType.MESH,
         )
 
@@ -69,9 +83,12 @@
 
     for device in (right, left, across, sib):
         greet(device)
-    for present, device in ((has_up, up), (has_dn, dn), (has_hi, hi), (has_lo, lo)):
+    others = (
+        (has_up, up), (has_dn, dn), (has_hi, hi), (has_lo, lo), (has_up2, up2), (has_dn2, dn2),
+    )
+    for present, device in others:
         pl.when(present)(lambda device=device: greet(device))
-    present_count = sum(x.astype(jnp.int32) for x in (has_up, has_dn, has_hi, has_lo))
+    present_count = sum(present.astype(jnp.int32) for present, _ in others)
 
     bulk_copy = pltpu.make_async_copy(sens.at[:, pl.ds(0, 2)], sv.at[:, pl.ds(0, 2)], lsem.at[NP])
 
@@ -90,19 +107,159 @@
         copy.start()
     bulk_copy.start()
     loop(NP, lambda p: shell_copy(p).start())
+    pl.semaphore_wait(barrier, 4 + present_count)
+
+    class Pair:
+        def __init__(self, number, srcs, dsts, slab):
+            plus, minus = (up, dn) if slab else (hi, lo)
+            self.to_plus, self.to_minus = (has_up, has_dn) if slab else (has_hi, has_lo)
+            self.a = remote(srcs[0], dsts[0], number, plus)
+            self.b = remote(srcs[1], dsts[1], number + 1, minus)
+
+        def start(self):
+            pl.when(self.to_plus)(lambda: self.a.start())
+            pl.when(self.to_minus)(lambda: self.b.start())
+
+        def wait_recv(self):
+            pl.when(self.to_minus)(lambda: self.a.wait_recv())
+            pl.when(self.to_plus)(lambda: self.b.wait_recv())
+
+        def wait_send(self):
+            pl.when(self.to_plus)(lambda: self.a.wait_send())
+            pl.when(self.to_minus)(lambda: self.b.wait_send())
+
+    halo_state = Pair(HS, (hsend, hsend), (hrecv.at[0], hrecv.at[1]), True)
+
+    class Halo:
+        def __init__(self, n, k, srcs):
+            base, target = ((X0, hx0), (X1, hx1))[n]
+            dsts = [target.at[d, pl.ds(2 * k, 2)] for d in range(2)]
+            self.direct = Pair(base + 2 * k, srcs, dsts, True)
+            self.k = k
+            if k < 3:
+                slot, arrival = relayed.at[n, k], RELAY + 3 * n + k
+                self.far = (
+                    remote(srcs[0], slot, base + 2 * k, up2, arrival),
+                    remote(srcs[1], slot, base + 2 * k + 1, dn2, arrival),
+                )
+                self.on = (
+                    remote(slot, dsts[0], arrival, dn, base + 2 * k),
+                    remote(slot, dsts[1], arrival, up, base + 2 * k + 1),
+                )
+
+        def start(self):
+            ways = ((has_up, relay_up, self.direct.a), (has_dn, relay_dn, self.direct.b))
+            for d, (present, count, copy) in enumerate(ways):
+                pl.when(present & (self.k >= count))(lambda copy=copy: copy.start())
+                if self.k < 3:
+                    pl.when(self.k < count)(lambda d=d: self.far[d].start())
+
+        def send_on(self):
+            @pl.when(self.k < relay_here)
+            def _():
+                self.far[0].wait_recv()
+                pl.when(odd)(lambda: self.on[0].start())
+                pl.when(jnp.logical_not(odd))(lambda: self.on[1].start())
+
+        def wait_recv(self):
+            self.direct.wait_recv()
+
+        def wait_send(self):
+            self.direct.wait_send()
+            if self.k < 3:
+                pl.when(self.k < relay_here)(lambda: self.on[0].wait_send())
+
+    def halo0(k):
+        two, bulk = pl.ds(2 * k, 2), pl.ds(0, 2)
+        return Halo(0, k, (sens.at[two, bulk, pl.ds(8, 4)], sens.at[two, bulk, pl.ds(0, 4)]))
+
+    def halo1(k):
+        two = pl.ds(2 * k, 2)
+        return Halo(1, k, (bb.at[two, :, pl.ds(8, 4)], bb.at[two, :, pl.ds(0, 4)]))
+
+    halos = [[halo0(k) for k in range(CHUNKS)], [halo1(k) for k in range(CHUNKS)]]
+    partial_state = Pair(RS, (rsend, rsend), (rrecv.at[0], rrecv.at[1]), True)
+    eight = pl.ds(0, NP)
+    rows0 = Pair(Y0, (yb0.at[0, eight], yb0.at[1, eight]), (yr0.at[0, eight], yr0.at[1, eight]), False)
+
+    def rows1(q):
+        return Pair(Y1 + 2 * q, (yb1.at[0, q], yb1.at[1, q]), (yr1.at[0, q], yr1.at[1, q]), False)
+
+    def shard(j, first, count):
+        return gst.at[pl.ds(first, count), pl.ds(j * 16, 16)]
+
+    rows0s = Pair(Y0S, (yb0.at[0, NP], yb0.at[1, NP]), (yr0.at[0, NP], yr0.at[1, NP]), False)
+
+    class Gather:
+        def __init__(self, first, count, number):
+            def messages(shards):
+                upper = count // 2
+                whole, a, b = (first, count), (first, count - upper), (first + count - upper, upper)
+                parts = (whole, whole, whole, a, whole, b, whole, a, b)
+                devices = (right, left, sib, right, sib, left, sib, sib, sib)
+                result = []
+                for k in range(9):
+                    ref = shard(shards[k], *parts[k])
+                    result.append(remote(ref, ref, number + k, devices[k]))
+                return result
+
+            self.sent = messages((me, me, me, jm, jm, jp, jp, jo, jo))
+            self.heard = messages(
+                (jm, jp, me + other, jo, jm + other, jo, jp + other, jo + other, jo + other)
+            )
+
+        def start(self):
+            for k in range(3):
+                self.sent[k].start()
+
+        def second(self):
+            for k in range(2):
+                self.heard[k].wait_recv()
+                self.sent[3 + 2 * k].start()
+                self.sent[4 + 2 * k].start()
+
+        def third(self):
+            for k in range(2):
+                self.heard[3 + 2 * k].wait_recv()
+                self.sent[7 + k].start()
+
+        def finish(self):
+            for k in (2, 4, 6, 7, 8):
+                self.heard[k].wait_recv()
+
+        def wait_send(self):
+            for message in self.sent:
+                message.wait_send()
+
+    sets = [Gather(first, count, GATHER + 9 * n) for n, (first, count) in enumerate(SETS)]
+
+    def direct_messages(shards):
+        devices = (right, left, across, sib, sib, sib, sib)
+        refs = [shard(j, NG - 1, 1) for j in shards]
+        return [remote(ref, ref, DIRECT + k, device) for k, (ref, device) in enumerate(zip(refs, devices))]
+
+    halo_sent = direct_messages((me, me, me, me, jm, jp, jo))
+    halo_heard = direct_messages((jm, jp, jo, me + other, jm + other, jp + other, jo + other))
+
     small[0].wait()
-
     mine = pl.multiple_of(me * 16, 16)
-    blank = jnp.zeros((16, 32), F32)
-    for g in range(11):
-        parts = [st_in[4 * g + k] if 4 * g + k < 42 else blank for k in range(4)]
-        gst[g, pl.ds(mine, 16), :] = jnp.concatenate(parts, axis=-1)
-    hsend[...] = jnp.concatenate([st_in[q] for q in (2, 5, 0, 3)], axis=-1)
-    wst[pl.ds(mine, 16), :] = jnp.concatenate(
-        [st_in[q] - st_in[r] for q, r in ((0, 21), (3, 39), (2, 23), (5, 41))], axis=-1
-    )
-    for copy in small[1:]:
-        copy.wait()
+    order = [3 * field + x for field in ORDER for x in range(3)]
+
+    def pack_group(planes):
+        blank = jnp.zeros((16, 32), F32)
+        return jnp.concatenate([blank if q is None else st_in[q] for q in planes], axis=-1)
+
+    def pack_set(n):
+        for g in range(SETS[n][0], min(SETS[n][0] + SETS[n][1], 11)):
+            gst[g, pl.ds(mine, 16), :] = pack_group((order + [None] * 2)[4 * g : 4 * g + 4])
+
+    pack_set(0)
+    sets[0].start()
+    hsend[...] = pack_group((2, 5, 0, 3))
+    halo_state.start()
+    pack_set(1)
+    sets[1].start()
+    halos[0][0].start()
 
     def zero_tables(b):
         nothing = jnp.zeros((8, 128), F32)
@@ -114,98 +271,8 @@
                     gv[n, b, k, f] = nothing
 
     loop(NB, zero_tables)
-
-    pl.semaphore_wait(barrier, 4 + present_count)
-
-    class Pair:
-        def __init__(self, number, srcs, dsts, slab):
-            plus, minus = (up, dn) if slab else (hi, lo)
-            self.to_plus, self.to_minus = (has_up, has_dn) if slab else (has_hi, has_lo)
-            self.a = remote(srcs[0], dsts[0], number, plus)
-            self.b = remote(srcs[1], dsts[1], number + 1, minus)
-
-        def start(self):
-            pl.when(self.to_plus)(lambda: self.a.start())
-            pl.when(self.to_minus)(lambda: self.b.start())
-
-        def wait_recv(self):
-            pl.when(self.to_minus)(lambda: self.a.wait_recv())
-            pl.when(self.to_plus)(lambda: self.b.wait_recv())
-
-        def wait_send(self):
-            pl.when(self.to_plus)(lambda: self.a.wait_send())
-            pl.when(self.to_minus)(lambda: self.b.wait_send())
-
-    halo_state = Pair(HS, (hsend, hsend), (hrecv.at[0], hrecv.at[1]), True)
-
-    def halo0(k):
-        two, bulk = pl.ds(2 * k, 2), pl.ds(0, 2)
-        return Pair(
-            X0 + 2 * k,
-            (sens.at[two, bulk, pl.ds(8, 4)], sens.at[two, bulk, pl.ds(0, 4)]),
-            (hx0.at[0, two], hx0.at[1, two]),
-            True,
-        )
-
-    def halo1(p):
-        return Pair(
-            X1 + 2 * p,
-            (bb.at[p, :, pl.ds(8, 4)], bb.at[p, :, pl.ds(0, 4)]),
-            (hx1.at[0, p], hx1.at[1, p]),
-            True,
-        )
-
-    partial_state = Pair(RS, (rsend, rsend), (rrecv.at[0], rrecv.at[1]), True)
-    eight = pl.ds(0, NP)
-    rows0 = Pair(Y0, (yb0.at[0, eight], yb0.at[1, eight]), (yr0.at[0, eight], yr0.at[1, eight]), False)
-
-    def rows1(q):
-        return Pair(Y1 + 2 * q, (yb1.at[0, q], yb1.at[1, q]), (yr1.at[0, q], yr1.at[1, q]), False)
-
-    def shard(j, first, count):
-        return gst.at[pl.ds(first, count), pl.ds(pl.multiple_of(j * 16, 16), 16)]
-
-    def pass_on(j, first, count, number, device):
-        ref = shard(j, first, count)
-        return remote(ref, ref, number, device)
-
-    send_a = [
-        pass_on(me, 0, 11, GA, right), pass_on(me, 0, 11, GA + 1, left), pass_on(me, 0, 11, GA + 2, sib),
-        pass_on(jm, 0, 6, GA + 3, right), pass_on(jm, 0, 11, GA + 4, sib),
-        pass_on(jp, 6, 5, GA + 5, left), pass_on(jp, 0, 11, GA + 6, sib),
-        pass_on(jo, 0, 6, GA + 7, sib), pass_on(jo, 6, 5, GA + 8, sib),
-    ]
-    recv_a = [
-        pass_on(jm, 0, 11, GA, right), pass_on(jp, 0, 11, GA + 1, left), pass_on(me + other, 0, 11, GA + 2, sib),
-        pass_on(jo, 0, 6, GA + 3, right), pass_on(jm + other, 0, 11, GA + 4, sib),
-        pass_on(jo, 6, 5, GA + 5, left), pass_on(jp + other, 0, 11, GA + 6, sib),
-        pass_on(jo + other, 0, 6, GA + 7, sib), pass_on(jo + other, 6, 5, GA + 8, sib),
-    ]
-    tile_state = Pair(YS, (shard(me, 0, 2), shard(me, 0, 2)), (tile_recv.at[0], tile_recv.at[1]), False)
-
-    def small_gather(ref_of, number):
-        def messages(shards):
-            devices = (right, left, across, sib, sib, sib, sib)
-            return [
-                remote(ref_of(j), ref_of(j), number + k, device)
-                for k, (j, device) in enumerate(zip(shards, devices))
-            ]
-
-        return (
-            messages((me, me, me, me, jm, jp, jo)),
-            messages((jm, jp, jo, me + other, jm + other, jp + other, jo + other)),
-        )
-
-    send_b, recv_b = small_gather(lambda j: shard(j, 11, 2), GB)
-    send_w, recv_w = small_gather(lambda j: wst.at[pl.ds(pl.multiple_of(j * 16, 16), 16)], GW)
-
-    for k in range(4):
-        send_w[k].start()
-    halo_state.start()
-    tile_state.start()
-    for k in range(3):
-        send_a[k].start()
-    loop(4, lambda k: halo0(k).start())
+    for copy in small[1:]:
+        copy.wait()
 
     def clear(ref, k):
         ref[k] = jnp.zeros(ref.shape[1:], F32)
@@ -222,7 +289,7 @@
     for absent, k in ((jnp.logical_not(has_lo), 0), (jnp.logical_not(has_hi), 1)):
         @pl.when(absent)
         def _(k=k):
-            for ref in (yr0, yr1, tile_recv):
+            for ref in (yr0, yr1):
                 clear(ref, k)
 
     def cell_theta(b):
@@ -258,30 +325,43 @@
 
     lane16 = lax.broadcasted_iota(jnp.int32, (16, 128), 1)
     halo_state.wait_recv()
-    gst[11, pl.ds(mine, 16), :] = jnp.where(lane16 < 64, hrecv[0], hrecv[1])
-    tile_state.wait_recv()
-    spot = lax.rem(lane16, 32)
-    gst[12, pl.ds(mine, 16), :] = jnp.where(
-        spot == 31,
-        tile_recv[0, 0],
-        jnp.where(
-            spot == 0,
-            tile_recv[1, 0],
-            jnp.where(spot == 30, pltpu.roll(tile_recv[0, 1], 127, 1), pltpu.roll(tile_recv[1, 1], 1, 1)),
-        ),
-    )
+    gst[NG - 1, pl.ds(mine, 16), :] = jnp.where(lane16 < 64, hrecv[0], hrecv[1])
     for k in range(4):
-        send_b[k].start()
+        halo_sent[k].start()
+    sets[0].second()
+    halos[0][1].start()
+    sets[1].second()
+    halos[0][2].start()
+    halos[0][3].start()
     for k in range(3):
-        recv_w[k].wait_recv()
-        send_w[4 + k].start()
-    recv_a[0].wait_recv()
-    send_a[3].start()
-    send_a[4].start()
-    recv_a[1].wait_recv()
-    send_a[5].start()
-    send_a[6].start()
-
+        halo_heard[k].wait_recv()
+        halo_sent[4 + k].start()
+    for gather in sets:
+        gather.third()
+    for gather in sets:
+        gather.finish()
+
+    def unpack(g):
+        s0[pl.ds(16 * g, 16)] = gst[g].T.reshape(16, 8, 128)
+
+    def bulk_forcing(n, state, first, count):
+        for i in range(2):
+            gap = state[pl.ds(i * NB + first, count)] - state[pl.ds((2 + i) * NB + first, count)]
+            gp[n, i, pl.ds(first, count)] = -(DT * pack[pl.ds(first, count)]) * gap
+
+    def state_rows(state, buffer):
+        for i in range(2):
+            for x in range(3):
+                r = 3 * i + x
+                buffer[0, NP, pl.ds(r, 1), :] = state[i * NB + 4 * x + 3, pl.ds(7, 1), :]
+                buffer[1, NP, pl.ds(r, 1), :] = state[i * NB + 4 * x, pl.ds(0, 1), :]
+
+    loop(NG - 1, unpack)
+    state_rows(s0, yb0)
+    rows0s.start()
+    bulk_forcing(0, s0, 0, NB)
+    for k in range(3):
+        halos[0][k].send_on()
     row = lax.broadcasted_iota(jnp.int32, (32, 128), 0)
     lane = lax.broadcasted_iota(jnp.int32, (32, 128), 1)
 
@@ -314,15 +394,9 @@
         target = jnp.where(lax.div(t, 8) == i, lax.rem(t, 8), -1)
         return jnp.where(zone[pl.ds(4 * x, 4)] == target, values, 0.0)
 
-    for k in range(3, 7):
-        recv_w[k].wait_recv()
-    turned = wst[...].T.reshape(2, 2, 4, 8, 128)
-    for k in range(2):
-        for i in range(2):
-            fw[k, i] = -(DT * pack[pl.ds(8 * k, 4)]) * turned[k, i]
     rows0.wait_recv()
 
-    def partial_and_send(p):
+    def partial(p):
         shell_copy(p).wait()
         for i in range(2):
             planes = [plane(sv[p, i, pl.ds(4 * x, 4)]) for x in range(3)]
@@ -331,37 +405,21 @@
                 lambda x: yr0[0, p, pl.ds(3 * i + x, 1), :], lambda x: yr0[1, p, pl.ds(3 * i + x, 1), :],
             )
             for x in range(3):
-                v = fresh[x].reshape(4, 8, 128)
-                if x != 1:
-                    v = v + forcing(p, i, x, fw[x // 2, i])
-                bb[p, i, pl.ds(4 * x, 4)] = v
-        halo1(p).start()
-
-    loop(NP, partial_and_send)
+                bb[p, i, pl.ds(4 * x, 4)] = fresh[x].reshape(4, 8, 128) + forcing(p, i, x, gp[0, i, pl.ds(4 * x, 4)])
 
     for k in range(3):
-        recv_b[k].wait_recv()
-        send_b[4 + k].start()
-    recv_a[3].wait_recv()
-    send_a[7].start()
-    recv_a[5].wait_recv()
-    send_a[8].start()
-    for k in (2, 4, 6, 7, 8):
-        recv_a[k].wait_recv()
+        loop(2, lambda j: partial(2 * k + j))
+        halos[1][k].start()
+
     for k in range(3, 7):
-        recv_b[k].wait_recv()
-
-    def unpack(g):
-        s0[pl.ds(16 * g, 16)] = gst[g].T.reshape(16, 8, 128)
-
-    loop(NG, unpack)
-
+        halo_heard[k].wait_recv()
+    unpack(NG - 1)
 
     def tables(n, now, later):
         def block(b):
             kf, dp, qm, bb_ = ([th[b, 2 * k + i] for i in range(2)] for k in range(4))
             conc = [now[i * NB + b] for i in range(2)]
-            pore = [[now[(2 + 6 * i + s) * NB + b] for s in range(6)] for i in range(2)]
+            pore = [[now[at(2 + 6 * i + s) + b] for s in range(6)] for i in range(2)]
             cap = [qm[i] * bb_[i] for i in range(2)]
             film = [FILM * kf[i] for i in range(2)]
             for s in range(6):
@@ -390,45 +448,41 @@
                     if s == 5:
                         gap = conc[i] - pore[i][5]
                         gv[n, b, i, f] = FILM * gap
-                        gp[n, i, b] = -(DT * pack[b]) * gap
                         fresh = fresh + film[i] * gap
-                    later[(2 + f) * NB + b] = fresh
+                    later[at(2 + f) + b] = fresh
 
         loop(NB, block)
 
     tables(0, s0, s1)
 
-    lower = ((31, 63, 95), (127, 30, 62))
-    upper = ((0, 32, 64), (96, 1, 33))
-
-    def turned_row(r):
-        return s0[192 + r // 8, pl.ds(r % 8, 1), :]
-
+    rows0s.wait_recv()
     for i in range(2):
         planes = [plane(s0[pl.ds(i * NB + 4 * x, 4)]) for x in range(3)]
         fresh = advance(
-            i, planes, lambda x: s0[pl.ds((7 + 6 * i) * NB + 4 * x, 4)],
-            lambda x: turned_row(lower[i][x]), lambda x: turned_row(upper[i][x]),
+            i, planes, lambda x: s0[pl.ds(at(7 + 6 * i) + 4 * x, 4)],
+            lambda x: yr0[0, NP, pl.ds(3 * i + x, 1), :], lambda x: yr0[1, NP, pl.ds(3 * i + x, 1), :],
         )
         bs[pl.ds(4 * i, 4)] = fresh[2].reshape(4, 8, 128)
         bs[pl.ds(8 + 4 * i, 4)] = fresh[0].reshape(4, 8, 128)
         s1[pl.ds(i * NB, 4)] = fresh[0].reshape(4, 8, 128) + BEHIND * s0[pl.ds(176 + 4 * i, 4)]
         s1[pl.ds(i * NB + 4, 4)] = fresh[1].reshape(4, 8, 128)
         s1[pl.ds(i * NB + 8, 4)] = fresh[2].reshape(4, 8, 128) + AHEAD * s0[pl.ds(184 + 4 * i, 4)]
-        for x in range(3):
-            r = 3 * i + x
-            yb1[0, NP, pl.ds(r, 1), :] = s1[i * NB + 4 * x + 3, pl.ds(7, 1), :]
-            yb1[1, NP, pl.ds(r, 1), :] = s1[i * NB + 4 * x, pl.ds(0, 1), :]
+    state_rows(s1, yb1)
     rows1(NP).start()
     turn[...] = bs[...].reshape(128, 128).T
     rsend[...] = turn[pl.ds(mine, 16), :]
     partial_state.start()
+    loop(2, lambda j: partial(6 + j))
+    halos[1][3].start()
+    halos[1][0].send_on()
+    bulk_forcing(1, s1, 0, NB)
     tables(1, s1, s2)
+    halos[1][1].send_on()
 
     def whole(p):
         for i in range(2):
             c1[p, i, pl.ds(0, 4)] = bb[p, i, pl.ds(0, 4)] + BEHIND * hx0[0, p, i]
-            c1[p, i, pl.ds(4, 4)] = bb[p, i, pl.ds(4, 4)] + forcing(p, i, 1, gp[0, i, pl.ds(4, 4)])
+            c1[p, i, pl.ds(4, 4)] = bb[p, i, pl.ds(4, 4)]
             c1[p, i, pl.ds(8, 4)] = bb[p, i, pl.ds(8, 4)] + AHEAD * hx0[1, p, i]
             for x in range(3):
                 r = 3 * i + x
@@ -469,13 +523,13 @@
 
         loop(NB, block)
 
-    def step_chunk(k):
-        halo0(k).wait_recv()
+    for k in range(CHUNKS):
+        halos[0][k].wait_recv()
         for j in range(2):
             whole(2 * k + j)
         loop(2, lambda j: shells(2 * k + j))
-
-    loop(4, step_chunk)
+        if k == 0:
+            halos[1][2].send_on()
 
     from_dn = (BEHIND * AHEAD) * has_dn.astype(F32)
     from_up = (BEHIND * AHEAD) * has_up.astype(F32)
@@ -499,7 +553,7 @@
     for i in range(2):
         planes = [plane(s1[pl.ds(i * NB + 4 * x, 4)]) for x in range(3)]
         fresh = advance(
-            i, planes, lambda x: s1[pl.ds((7 + 6 * i) * NB + 4 * x, 4)],
+            i, planes, lambda x: s1[pl.ds(at(7 + 6 * i) + 4 * x, 4)],
             lambda x: yr1[0, NP, pl.ds(3 * i + x, 1), :], lambda x: yr1[1, NP, pl.ds(3 * i + x, 1), :],
         )
         fresh[0] = fresh[0] + from_dn * plane(s0[pl.ds(i * NB, 4)])
@@ -519,24 +573,27 @@
             own = own + jnp.where((lane16 >= 32) & (lane16 < 64), AHEAD * rolled, 0.0)
         for k in range(4):
             if 4 * g + k < 42:
-                st_out[4 * g + k] = own[:, 32 * k : 32 * k + 32]
+                st_out[order[4 * g + k]] = own[:, 32 * k : 32 * k + 32]
 
     def last(p):
-        halo1(p).wait_recv()
         for i in range(2):
             out[p, i, pl.ds(0, 4)] = out[p, i, pl.ds(0, 4)] + BEHIND * hx1[0, p, i]
             out[p, i, pl.ds(8, 4)] = out[p, i, pl.ds(8, 4)] + AHEAD * hx1[1, p, i]
 
-    loop(NP, last)
+    for k in range(CHUNKS):
+        halos[1][k].wait_recv()
+        loop(2, lambda j: last(2 * k + j))
 
     halo_state.wait_send()
     partial_state.wait_send()
     rows0.wait_send()
-    tile_state.wait_send()
-    loop(4, lambda k: halo0(k).wait_send())
-    loop(NP, lambda p: halo1(p).wait_send())
+    rows0s.wait_send()
+    for halo in halos[0] + halos[1]:
+        halo.wait_send()
     loop(NP + 1, lambda q: rows1(q).wait_send())
-    for message in send_a + send_b + send_w:
+    for gather in sets:
+        gather.wait_send()
+    for message in halo_sent:
         message.wait_send()
 
 
@@ -556,16 +613,16 @@
     anywhere = pl.BlockSpec(memory_space=pl.ANY)
     scratch = [
         (NP, 14, NB, 8, 128),
-        (NG, 128, 128), (128, 128),
-        (16, 128), (2, 16, 128), (2, 2, 16, 128),
+        (NG, 128, 128),
+        (16, 128), (2, 16, 128),
         (16, 128), (2, 16, 128), (128, 128),
-        (208, 8, 128), (168, 8, 128), (176, 8, 128),
+        (192, 8, 128), (168, 8, 128), (176, 8, 128),
         (NB, 8, 8, 128), (NB, 10, 8, 128), (2, NB, 8, 128), (2, NB, 8, 128),
         (2, NB, 12, 8, 128), (2, NB, 12, 8, 128), (2, NB, 8, 12, 8, 128),
-        (2, 2, NB, 8, 128), (2, 2, 4, 8, 128),
-        (2, NP, 2, 4, 8, 128), (2, NP, 2, 4, 8, 128),
+        (2, 2, NB, 8, 128),
+        (2, NP, 2, 4, 8, 128), (2, NP, 2, 4, 8, 128), (2, 3, 2, 2, 4, 8, 128),
         (NP, 2, NB, 8, 128), (16, 8, 128), (NP, 2, NB, 8, 128), (NP, 2, NB, 8, 128),
-        (2, NP, 8, 128), (2, NP, 8, 128), (2, NP + 1, 8, 128), (2, NP + 1, 8, 128),
+        (2, NP + 1, 8, 128), (2, NP + 1, 8, 128), (2, NP + 1, 8, 128), (2, NP + 1, 8, 128),
         (42, 16, 32), (NB, 8, 128),
     ]
     new_state, new_sens = pl.pallas_call(

time: 45.5 us -> 41.8 us (0.919)
  Pallas kernels: 44.7 us -> 40.9 us
    pallas_call x1, Pallas kernels: 42.1 us -> 38.3 us  [shards(): pl.pallas_call(kernel, out_shape=(jax.ShapeDtypeStruct((42, 16, 32), F32)...]
where the time goes in v3:
time: 41.8 us; the launch traced here: 41.5 us
  Pallas kernels  40.9 us (98%)
  between operations  0.64 us (2%)
    pallas_call x1, Pallas kernels, shards(): pl.pallas_call(kernel, out_shape=(jax.ShapeDtypeStruct((42, 16, 32), F32)...  38.3 us
    pallas_call x1, Pallas kernels, shards(): pl.pallas_call(write_out, out_shape=(jax.ShapeDtypeStruct((42, 16, 32), F...  2.61 us

profile of v3, /device:TPU:1, one launch (start us, length us, event | category | flops | bytes accessed | tf_op | source)
XLA Modules:
  0.0 41.5 jit_solution(14139809604545272244)
XLA Ops:
  0.6 38.3 %column.1 = (f32[42,16,32]{2,1,0:T(8,128)S(1)}, f32[8,14,12,8,128]{4,3,2,1,0:T(8,128)S(1)}) custom-call(f32[42,16,32]{2,1,0:T(8,128)} %bitcast.11, f32[8,14,12,8,128]{4,3,2,1,0:T(8,128)} %bitcast.10, f32[12,8,128]{2,1,0:T(8,128)} %bitcast.12, s32[12,8,128]{2,1,0:T(8,128)} %bitcast.13, f32[8,8]{1,0:T(8,128)} %coef_arg.1, s32[8]{0:T(128)} %targ_arg.1), custom_call_target="tpu_custom_call" | custom-call | tf_op jit(solution)/shard_map/column/pallas_call | solution.py:628
  38.9 2.6 %write_out.1 = (f32[42,16,32]{2,1,0:T(8,128)}, f32[8,14,12,8,128]{4,3,2,1,0:T(8,128)}) custom-call(f32[42,16,32]{2,1,0:T(8,128)S(1)} %get-tuple-element.6.st, f32[8,14,12,8,128]{4,3,2,1,0:T(8,128)S(1)} %get-tuple-element.7.sens), custom_call_target="tpu_custom_call" | custom-call | tf_op jit(solution)/shard_map/write_out/pallas_call | solution.py:662

commit v4 on v3

--- a/solution.py
+++ b/solution.py
@@ -18,8 +18,9 @@
 NB = 12
 NG = 12
 ORDER = (0, 1, 7, 13, 2, 3, 4, 5, 6, 8, 9, 10, 11, 12)
-SETS = ((0, 6), (6, 5))
-CHUNKS = 4
+SETS = ((0, 6), (6, 6))
+CHUNKS = 8
+VIA = 6
 
 X0 = 0
 X1 = X0 + 2 * CHUNKS
@@ -30,8 +31,7 @@
 Y1 = Y0S + 2
 GATHER = Y1 + 18
 RELAY = GATHER + 9 * len(SETS)
-DIRECT = RELAY + 6
-MESSAGES = DIRECT + 7
+MESSAGES = RELAY + 2 * VIA
 SMALL = NP + 1
 LOCAL = SMALL + 5
 
@@ -58,13 +58,13 @@
     has_lo, has_hi = ti > 0, ti < 3
     up, dn = (me, sl + 1, ti), (me, sl - 1, ti)
     hi, lo = (me, sl, ti + 1), (me, sl, ti - 1)
-    right, left, across, sib = (jp, sl, ti), (jm, sl, ti), (jo, sl, ti), (me + other, sl, ti)
+    right, left, sib = (jp, sl, ti), (jm, sl, ti), (me + other, sl, ti)
     up2, dn2 = (me, sl + 2, ti), (me, sl - 2, ti)
     has_dn2, has_up2 = sl > 1, sl < 6
     half, odd = lax.div(sl, 2), lax.rem(sl, 2) == 1
-    relay_up = jnp.where(odd & has_up, half + 1, 0)
-    relay_dn = jnp.where(jnp.logical_not(odd) & has_dn, 4 - half, 0)
-    relay_here = jnp.where(odd, half, jnp.maximum(3 - half, 0))
+    relay_up = jnp.where(odd & has_up, 2 * half + 2, 0)
+    relay_dn = jnp.where(jnp.logical_not(odd) & has_dn, 8 - 2 * half, 0)
+    relay_here = jnp.where(odd, 2 * half, jnp.maximum(6 - 2 * half, 0))
 
     def loop(n, body):
         lax.fori_loop(0, n, lambda i, carry: (body(i), carry)[1], 0)
@@ -81,7 +81,7 @@
     def greet(device):
         pl.semaphore_signal(barrier, inc=1, device_id=device, device_id_type=pl.DeviceIdType.MESH)
 
-    for device in (right, left, across, sib):
+    for device in (right, left, sib):
         greet(device)
     others = (
         (has_up, up), (has_dn, dn), (has_hi, hi), (has_lo, lo), (has_up2, up2), (has_dn2, dn2),
@@ -105,9 +105,22 @@
     ]
     for copy in small:
         copy.start()
-    bulk_copy.start()
-    loop(NP, lambda p: shell_copy(p).start())
-    pl.semaphore_wait(barrier, 4 + present_count)
+    small[0].wait()
+    mine = pl.multiple_of(me * 16, 16)
+    order = [3 * field + x for field in ORDER for x in range(3)]
+
+    def pack_group(planes):
+        blank = jnp.zeros((16, 32), F32)
+        return jnp.concatenate([blank if q is None else st_in[q] for q in planes], axis=-1)
+
+    def pack_set(n):
+        for g in range(SETS[n][0], min(SETS[n][0] + SETS[n][1], 11)):
+            gst[g, pl.ds(mine, 16), :] = pack_group((order + [None] * 2)[4 * g : 4 * g + 4])
+
+    pack_set(0)
+    hsend[...] = pack_group((2, 5, 0, 3))
+
+    pl.semaphore_wait(barrier, 3 + present_count)
 
     class Pair:
         def __init__(self, number, srcs, dsts, slab):
@@ -133,11 +146,11 @@
     class Halo:
         def __init__(self, n, k, srcs):
             base, target = ((X0, hx0), (X1, hx1))[n]
-            dsts = [target.at[d, pl.ds(2 * k, 2)] for d in range(2)]
+            dsts = [target.at[d, k] for d in range(2)]
             self.direct = Pair(base + 2 * k, srcs, dsts, True)
             self.k = k
-            if k < 3:
-                slot, arrival = relayed.at[n, k], RELAY + 3 * n + k
+            if k < VIA:
+                slot, arrival = relayed.at[n, k], RELAY + VIA * n + k
                 self.far = (
                     remote(srcs[0], slot, base + 2 * k, up2, arrival),
                     remote(srcs[1], slot, base + 2 * k + 1, dn2, arrival),
@@ -151,7 +164,7 @@
             ways = ((has_up, relay_up, self.direct.a), (has_dn, relay_dn, self.direct.b))
             for d, (present, count, copy) in enumerate(ways):
                 pl.when(present & (self.k >= count))(lambda copy=copy: copy.start())
-                if self.k < 3:
+                if self.k < VIA:
                     pl.when(self.k < count)(lambda d=d: self.far[d].start())
 
         def send_on(self):
@@ -166,16 +179,15 @@
 
         def wait_send(self):
             self.direct.wait_send()
-            if self.k < 3:
+            if self.k < VIA:
                 pl.when(self.k < relay_here)(lambda: self.on[0].wait_send())
 
     def halo0(k):
-        two, bulk = pl.ds(2 * k, 2), pl.ds(0, 2)
-        return Halo(0, k, (sens.at[two, bulk, pl.ds(8, 4)], sens.at[two, bulk, pl.ds(0, 4)]))
+        bulk = pl.ds(0, 2)
+        return Halo(0, k, (sens.at[k, bulk, pl.ds(8, 4)], sens.at[k, bulk, pl.ds(0, 4)]))
 
     def halo1(k):
-        two = pl.ds(2 * k, 2)
-        return Halo(1, k, (bb.at[two, :, pl.ds(8, 4)], bb.at[two, :, pl.ds(0, 4)]))
+        return Halo(1, k, (bb.at[k, :, pl.ds(8, 4)], bb.at[k, :, pl.ds(0, 4)]))
 
     halos = [[halo0(k) for k in range(CHUNKS)], [halo1(k) for k in range(CHUNKS)]]
     partial_state = Pair(RS, (rsend, rsend), (rrecv.at[0], rrecv.at[1]), True)
@@ -233,33 +245,11 @@
 
     sets = [Gather(first, count, GATHER + 9 * n) for n, (first, count) in enumerate(SETS)]
 
-    def direct_messages(shards):
-        devices = (right, left, across, sib, sib, sib, sib)
-        refs = [shard(j, NG - 1, 1) for j in shards]
-        return [remote(ref, ref, DIRECT + k, device) for k, (ref, device) in enumerate(zip(refs, devices))]
-
-    halo_sent = direct_messages((me, me, me, me, jm, jp, jo))
-    halo_heard = direct_messages((jm, jp, jo, me + other, jm + other, jp + other, jo + other))
-
-    small[0].wait()
-    mine = pl.multiple_of(me * 16, 16)
-    order = [3 * field + x for field in ORDER for x in range(3)]
-
-    def pack_group(planes):
-        blank = jnp.zeros((16, 32), F32)
-        return jnp.concatenate([blank if q is None else st_in[q] for q in planes], axis=-1)
-
-    def pack_set(n):
-        for g in range(SETS[n][0], min(SETS[n][0] + SETS[n][1], 11)):
-            gst[g, pl.ds(mine, 16), :] = pack_group((order + [None] * 2)[4 * g : 4 * g + 4])
-
-    pack_set(0)
+    halo_state.start()
     sets[0].start()
-    hsend[...] = pack_group((2, 5, 0, 3))
-    halo_state.start()
+    bulk_copy.start()
+    loop(NP, lambda p: shell_copy(p).start())
     pack_set(1)
-    sets[1].start()
-    halos[0][0].start()
 
     def zero_tables(b):
         nothing = jnp.zeros((8, 128), F32)
@@ -323,45 +313,6 @@
     loop(NP, pack_rows0)
     rows0.start()
 
-    lane16 = lax.broadcasted_iota(jnp.int32, (16, 128), 1)
-    halo_state.wait_recv()
-    gst[NG - 1, pl.ds(mine, 16), :] = jnp.where(lane16 < 64, hrecv[0], hrecv[1])
-    for k in range(4):
-        halo_sent[k].start()
-    sets[0].second()
-    halos[0][1].start()
-    sets[1].second()
-    halos[0][2].start()
-    halos[0][3].start()
-    for k in range(3):
-        halo_heard[k].wait_recv()
-        halo_sent[4 + k].start()
-    for gather in sets:
-        gather.third()
-    for gather in sets:
-        gather.finish()
-
-    def unpack(g):
-        s0[pl.ds(16 * g, 16)] = gst[g].T.reshape(16, 8, 128)
-
-    def bulk_forcing(n, state, first, count):
-        for i in range(2):
-            gap = state[pl.ds(i * NB + first, count)] - state[pl.ds((2 + i) * NB + first, count)]
-            gp[n, i, pl.ds(first, count)] = -(DT * pack[pl.ds(first, count)]) * gap
-
-    def state_rows(state, buffer):
-        for i in range(2):
-            for x in range(3):
-                r = 3 * i + x
-                buffer[0, NP, pl.ds(r, 1), :] = state[i * NB + 4 * x + 3, pl.ds(7, 1), :]
-                buffer[1, NP, pl.ds(r, 1), :] = state[i * NB + 4 * x, pl.ds(0, 1), :]
-
-    loop(NG - 1, unpack)
-    state_rows(s0, yb0)
-    rows0s.start()
-    bulk_forcing(0, s0, 0, NB)
-    for k in range(3):
-        halos[0][k].send_on()
     row = lax.broadcasted_iota(jnp.int32, (32, 128), 0)
     lane = lax.broadcasted_iota(jnp.int32, (32, 128), 1)
 
@@ -389,12 +340,10 @@
             result.append(w)
         return result
 
-    def forcing(p, i, x, values):
+    def forcing(p, i, values):
         t = targ[p]
         target = jnp.where(lax.div(t, 8) == i, lax.rem(t, 8), -1)
-        return jnp.where(zone[pl.ds(4 * x, 4)] == target, values, 0.0)
-
-    rows0.wait_recv()
+        return jnp.where(zone[...] == target, values, 0.0)
 
     def partial(p):
         shell_copy(p).wait()
@@ -405,15 +354,58 @@
                 lambda x: yr0[0, p, pl.ds(3 * i + x, 1), :], lambda x: yr0[1, p, pl.ds(3 * i + x, 1), :],
             )
             for x in range(3):
-                bb[p, i, pl.ds(4 * x, 4)] = fresh[x].reshape(4, 8, 128) + forcing(p, i, x, gp[0, i, pl.ds(4 * x, 4)])
-
-    for k in range(3):
-        loop(2, lambda j: partial(2 * k + j))
+                bb[p, i, pl.ds(4 * x, 4)] = fresh[x].reshape(4, 8, 128)
+
+    lane16 = lax.broadcasted_iota(jnp.int32, (16, 128), 1)
+    halo_state.wait_recv()
+    gst[NG - 1, pl.ds(mine, 16), :] = jnp.where(lane16 < 64, hrecv[0], hrecv[1])
+    sets[1].start()
+    halos[0][0].start()
+    sets[0].second()
+    halos[0][1].start()
+    sets[1].second()
+    halos[0][2].start()
+    halos[0][3].start()
+    halos[0][4].start()
+    halos[0][5].start()
+    halos[0][6].start()
+    halos[0][7].start()
+    rows0.wait_recv()
+    loop(NP, partial)
+    for gather in sets:
+        gather.third()
+    for gather in sets:
+        gather.finish()
+
+    def unpack(g):
+        s0[pl.ds(16 * g, 16)] = gst[g].T.reshape(16, 8, 128)
+
+    def bulk_forcing(n, state, first, count):
+        for i in range(2):
+            gap = state[pl.ds(i * NB + first, count)] - state[pl.ds((2 + i) * NB + first, count)]
+            gp[n, i, pl.ds(first, count)] = -(DT * pack[pl.ds(first, count)]) * gap
+
+    def state_rows(state, buffer):
+        for i in range(2):
+            for x in range(3):
+                r = 3 * i + x
+                buffer[0, NP, pl.ds(r, 1), :] = state[i * NB + 4 * x + 3, pl.ds(7, 1), :]
+                buffer[1, NP, pl.ds(r, 1), :] = state[i * NB + 4 * x, pl.ds(0, 1), :]
+
+    loop(NG, unpack)
+    state_rows(s0, yb0)
+    rows0s.start()
+    bulk_forcing(0, s0, 0, NB)
+    for k in range(VIA):
+        halos[0][k].send_on()
+    def force(p):
+        for i in range(2):
+            bb[p, i] = bb[p, i] + forcing(p, i, gp[0, i])
+
+    for k in range(6):
+        force(k)
         halos[1][k].start()
 
-    for k in range(3, 7):
-        halo_heard[k].wait_recv()
-    unpack(NG - 1)
 
     def tables(n, now, later):
         def block(b):
@@ -472,12 +464,15 @@
     turn[...] = bs[...].reshape(128, 128).T
     rsend[...] = turn[pl.ds(mine, 16), :]
     partial_state.start()
-    loop(2, lambda j: partial(6 + j))
-    halos[1][3].start()
+    for k in range(6, CHUNKS):
+        force(k)
+        halos[1][k].start()
     halos[1][0].send_on()
+    halos[1][1].send_on()
     bulk_forcing(1, s1, 0, NB)
     tables(1, s1, s2)
-    halos[1][1].send_on()
+    halos[1][2].send_on()
+    halos[1][3].send_on()
 
     def whole(p):
         for i in range(2):
@@ -523,13 +518,13 @@
 
         loop(NB, block)
 
-    for k in range(CHUNKS):
-        halos[0][k].wait_recv()
+    for k in range(4):
         for j in range(2):
+            halos[0][2 * k + j].wait_recv()
             whole(2 * k + j)
         loop(2, lambda j: shells(2 * k + j))
-        if k == 0:
-            halos[1][2].send_on()
+        if k < 2:
+            halos[1][4 + k].send_on()
 
     from_dn = (BEHIND * AHEAD) * has_dn.astype(F32)
     from_up = (BEHIND * AHEAD) * has_up.astype(F32)
@@ -544,8 +539,9 @@
             )
             fresh[0] = fresh[0] + from_dn * plane(sv[p, i, pl.ds(0, 4)])
             fresh[2] = fresh[2] + from_up * plane(sv[p, i, pl.ds(8, 4)])
+            force_now = forcing(p, i, gp[1, i])
             for x in range(3):
-                out[p, i, pl.ds(4 * x, 4)] = fresh[x].reshape(4, 8, 128) + forcing(p, i, x, gp[1, i, pl.ds(4 * x, 4)])
+                out[p, i, pl.ds(4 * x, 4)] = fresh[x].reshape(4, 8, 128) + force_now[4 * x : 4 * x + 4]
 
     loop(NP, second)
 
@@ -582,7 +578,7 @@
 
     for k in range(CHUNKS):
         halos[1][k].wait_recv()
-        loop(2, lambda j: last(2 * k + j))
+        last(k)
 
     halo_state.wait_send()
     partial_state.wait_send()
@@ -593,8 +589,6 @@
     loop(NP + 1, lambda q: rows1(q).wait_send())
     for gather in sets:
         gather.wait_send()
-    for message in halo_sent:
-        message.wait_send()
 
 
 def write_out(st, sens, st_out, out, sems):
@@ -620,7 +614,7 @@
         (NB, 8, 8, 128), (NB, 10, 8, 128), (2, NB, 8, 128), (2, NB, 8, 128),
         (2, NB, 12, 8, 128), (2, NB, 12, 8, 128), (2, NB, 8, 12, 8, 128),
         (2, 2, NB, 8, 128),
-        (2, NP, 2, 4, 8, 128), (2, NP, 2, 4, 8, 128), (2, 3, 2, 2, 4, 8, 128),
+        (2, NP, 2, 4, 8, 128), (2, NP, 2, 4, 8, 128), (2, VIA, 2, 4, 8, 128),
         (NP, 2, NB, 8, 128), (16, 8, 128), (NP, 2, NB, 8, 128), (NP, 2, NB, 8, 128),
         (2, NP + 1, 8, 128), (2, NP + 1, 8, 128), (2, NP + 1, 8, 128), (2, NP + 1, 8, 128),
         (42, 16, 32), (NB, 8, 128),

time: 41.8 us -> 41 us (0.981)
  Pallas kernels: 40.9 us -> 40.2 us
    pallas_call x1, Pallas kernels: 38.3 us -> 37.6 us  [shards(): pl.pallas_call(kernel, out_shape=(jax.ShapeDtypeStruct((42, 16, 32), F32)...]
where the time goes in v4:
time: 41 us; the launch traced here: 40.9 us
  Pallas kernels  40.2 us (98%)
  between operations  0.64 us (2%)
    pallas_call x1, Pallas kernels, shards(): pl.pallas_call(kernel, out_shape=(jax.ShapeDtypeStruct((42, 16, 32), F32)...  37.6 us
    pallas_call x1, Pallas kernels, shards(): pl.pallas_call(write_out, out_shape=(jax.ShapeDtypeStruct((42, 16, 32), F...  2.61 us

profile of v4, /device:TPU:1, one launch (start us, length us, event | category | flops | bytes accessed | tf_op | source)
XLA Modules:
  0.0 40.9 jit_solution(12413061034855411543)
XLA Ops:
  0.6 37.6 %column.1 = (f32[42,16,32]{2,1,0:T(8,128)S(1)}, f32[8,14,12,8,128]{4,3,2,1,0:T(8,128)S(1)}) custom-call(f32[42,16,32]{2,1,0:T(8,128)} %bitcast.11, f32[8,14,12,8,128]{4,3,2,1,0:T(8,128)} %bitcast.10, f32[12,8,128]{2,1,0:T(8,128)} %bitcast.12, s32[12,8,128]{2,1,0:T(8,128)} %bitcast.13, f32[8,8]{1,0:T(8,128)} %coef_arg.1, s32[8]{0:T(128)} %targ_arg.1), custom_call_target="tpu_custom_call" | custom-call | tf_op jit(solution)/shard_map/column/pallas_call | solution.py:622
  38.3 2.6 %write_out.1 = (f32[42,16,32]{2,1,0:T(8,128)}, f32[8,14,12,8,128]{4,3,2,1,0:T(8,128)}) custom-call(f32[42,16,32]{2,1,0:T(8,128)S(1)} %get-tuple-element.6.st, f32[8,14,12,8,128]{4,3,2,1,0:T(8,128)S(1)} %get-tuple-element.7.sens), custom_call_target="tpu_custom_call" | custom-call | tf_op jit(solution)/shard_map/write_out/pallas_call | solution.py:656

commit v5 on v4

--- a/solution.py
+++ b/solution.py
@@ -576,19 +576,21 @@
             out[p, i, pl.ds(0, 4)] = out[p, i, pl.ds(0, 4)] + BEHIND * hx1[0, p, i]
             out[p, i, pl.ds(8, 4)] = out[p, i, pl.ds(8, 4)] + AHEAD * hx1[1, p, i]
 
-    for k in range(CHUNKS):
-        halos[1][k].wait_recv()
-        last(k)
-
     halo_state.wait_send()
-    partial_state.wait_send()
     rows0.wait_send()
     rows0s.wait_send()
-    for halo in halos[0] + halos[1]:
+    for halo in halos[0]:
         halo.wait_send()
     loop(NP + 1, lambda q: rows1(q).wait_send())
     for gather in sets:
         gather.wait_send()
+
+    for k in range(CHUNKS):
+        halos[1][k].wait_recv()
+        last(k)
+    for halo in halos[1]:
+        halo.wait_send()
+    partial_state.wait_send()
 
 
 def write_out(st, sens, st_out, out, sems):

time: 41 us -> 40.9 us (level)
  no operation moved by 1% of the time
where the time goes in v5:
time: 40.9 us; the launch traced here: 40.8 us
  Pallas kernels  40.2 us (98%)
  between operations  0.64 us (2%)
    pallas_call x1, Pallas kernels, shards(): pl.pallas_call(kernel, out_shape=(jax.ShapeDtypeStruct((42, 16, 32), F32)...  37.6 us
    pallas_call x1, Pallas kernels, shards(): pl.pallas_call(write_out, out_shape=(jax.ShapeDtypeStruct((42, 16, 32), F...  2.61 us

profile of v5, /device:TPU:1, one launch (start us, length us, event | category | flops | bytes accessed | tf_op | source)
XLA Modules:
  0.0 40.8 jit_solution(11300808260914467806)
XLA Ops:
  0.6 37.6 %column.1 = (f32[42,16,32]{2,1,0:T(8,128)S(1)}, f32[8,14,12,8,128]{4,3,2,1,0:T(8,128)S(1)}) custom-call(f32[42,16,32]{2,1,0:T(8,128)} %bitcast.11, f32[8,14,12,8,128]{4,3,2,1,0:T(8,128)} %bitcast.10, f32[12,8,128]{2,1,0:T(8,128)} %bitcast.12, s32[12,8,128]{2,1,0:T(8,128)} %bitcast.13, f32[8,8]{1,0:T(8,128)} %coef_arg.1, s32[8]{0:T(128)} %targ_arg.1), custom_call_target="tpu_custom_call" | custom-call | tf_op jit(solution)/shard_map/column/pallas_call | solution.py:624
  38.2 2.6 %write_out.1 = (f32[42,16,32]{2,1,0:T(8,128)}, f32[8,14,12,8,128]{4,3,2,1,0:T(8,128)}) custom-call(f32[42,16,32]{2,1,0:T(8,128)S(1)} %get-tuple-element.6.st, f32[8,14,12,8,128]{4,3,2,1,0:T(8,128)S(1)} %get-tuple-element.7.sens), custom_call_target="tpu_custom_call" | custom-call | tf_op jit(solution)/shard_map/write_out/pallas_call | solution.py:658

commit v6 on v5

--- a/solution.py
+++ b/solution.py
@@ -18,7 +18,7 @@
 NB = 12
 NG = 12
 ORDER = (0, 1, 7, 13, 2, 3, 4, 5, 6, 8, 9, 10, 11, 12)
-SETS = ((0, 6), (6, 6))
+SETS = ((0, 8), (8, 4))
 CHUNKS = 8
 VIA = 6
 

time: 40.9 us -> 40.6 us (level); the launches traced: 40.8 us -> 39.9 us
  Pallas kernels: 40.2 us -> 39.3 us
    pallas_call x1, Pallas kernels: 37.6 us -> 36.7 us  [shards(): pl.pallas_call(kernel, out_shape=(jax.ShapeDtypeStruct((42, 16, 32), F32)...]
where the time goes in v6:
time: 40.6 us; the launch traced here: 39.9 us
  Pallas kernels  39.3 us (97%)
  between operations  0.64 us (2%)
    pallas_call x1, Pallas kernels, shards(): pl.pallas_call(kernel, out_shape=(jax.ShapeDtypeStruct((42, 16, 32), F32)...  36.7 us
    pallas_call x1, Pallas kernels, shards(): pl.pallas_call(write_out, out_shape=(jax.ShapeDtypeStruct((42, 16, 32), F...  2.61 us

profile of v6, /device:TPU:1, one launch (start us, length us, event | category | flops | bytes accessed | tf_op | source)
XLA Modules:
  0.0 39.9 jit_solution(10887012779738230564)
XLA Ops:
  0.6 36.7 %column.1 = (f32[42,16,32]{2,1,0:T(8,128)S(1)}, f32[8,14,12,8,128]{4,3,2,1,0:T(8,128)S(1)}) custom-call(f32[42,16,32]{2,1,0:T(8,128)} %bitcast.11, f32[8,14,12,8,128]{4,3,2,1,0:T(8,128)} %bitcast.10, f32[12,8,128]{2,1,0:T(8,128)} %bitcast.12, s32[12,8,128]{2,1,0:T(8,128)} %bitcast.13, f32[8,8]{1,0:T(8,128)} %coef_arg.1, s32[8]{0:T(128)} %targ_arg.1), custom_call_target="tpu_custom_call" | custom-call | tf_op jit(solution)/shard_map/column/pallas_call | solution.py:624
  37.3 2.6 %write_out.1 = (f32[42,16,32]{2,1,0:T(8,128)}, f32[8,14,12,8,128]{4,3,2,1,0:T(8,128)}) custom-call(f32[42,16,32]{2,1,0:T(8,128)S(1)} %get-tuple-element.6.st, f32[8,14,12,8,128]{4,3,2,1,0:T(8,128)S(1)} %get-tuple-element.7.sens), custom_call_target="tpu_custom_call" | custom-call | tf_op jit(solution)/shard_map/write_out/pallas_call | solution.py:658
